TPU v7x, 256 devices: a whole 4x4x8 slice. The times are simulated.
256 devices in a mesh: seg: 8 (over x, y_hi), space: 32 (over z, y_lo, core).
Axes of the slice: x: 4, y: 4 (y_hi: 2, y_lo: 2; y = y_hi * 2 + y_lo), z: 8, core: 2. Of those that a mesh axis runs over, the one named last changes fastest.
Arguments:
- initial_states: float32 [8, 256, 512], P('seg', 'space'), may hold values from -6 to 6
- w_lift: bfloat16 [3, 3, 1, 32], replicated, may hold values from -2.1 to 2.1
- w_second: bfloat16 [3, 3, 32, 32], replicated, may hold values from -0.7 to 0.7
- w_third: bfloat16 [3, 3, 32, 32], replicated, may hold values from -0.7 to 0.7
- w_project: bfloat16 [3, 3, 32, 1], replicated, may hold values from -0.63 to 0.63
- shift_cells: int32 [8], P('seg'), may hold values from 0 to 511
- wavenumber: int32 [2], replicated, may hold values from 1 to 31
Outputs:
- updated: float32 [8, 256, 512], P('seg', 'space')
- mismatch: float32 [8, 256, 512], P('seg', 'space')
Inputs may be any that keep to these rules, and one draw needn't show every extreme that they name: `shift_cells`: column shifts between consecutive segments.
All inputs are finite; a program needn't handle non-finite values.
Results may differ from a plain program's by a relative error of at most 0.015.
Values may be sent and summed in bfloat16 or wider, within the bound.
No kernel may reach another device: no remote copies, remote signals or barrier semaphores. Data moves between devices by JAX's collectives and lax.ppermute only.
A program may use at most 64 MiB of HBM per device.

v0:
```python
import functools
import math

import jax
import jax.numpy as jnp
from jax import lax
from jax.experimental import pallas as pl
from jax.experimental.pallas import tpu as pltpu
from jax.sharding import PartitionSpec as P


time_step = 0.4
drag_rate = 0.1
learn_rate = 0.5

ROWS = 8
LANES = 128
COLS = 512
f32 = jnp.float32
bf16 = jnp.bfloat16


def groups_of(count, most=4):
    start = 0
    while start < count:
        size = min(most, count - start)
        yield start, size
        start += size


def slot_iota(shape):
    return lax.broadcasted_iota(jnp.int32, shape, len(shape) - 2)


def widened(field):
    slot = slot_iota(field.shape)
    moved = pltpu.roll(field, 4, 0)
    left = pltpu.roll(moved, 1, 1)
    right = pltpu.roll(moved, LANES - 1, 1)
    zero = jnp.zeros_like(field)
    return jnp.where((slot >= 1) & (slot <= 4), field, jnp.where(slot == 0, left, jnp.where(slot == 5, right, zero)))


def folded(partial):
    slot = slot_iota(partial.shape)
    moved = pltpu.roll(partial, 4, 0)
    left = pltpu.roll(moved, LANES - 1, 1)
    right = pltpu.roll(moved, 1, 1)
    return partial + jnp.where(slot == 4, left, jnp.where(slot == 1, right, jnp.zeros_like(partial)))


def put(dst, row, values):
    cut = values.reshape(2, 4 * 32, LANES)
    dst[row : row + 2, 32:160, :] = cut.astype(bf16)
    before = pltpu.roll(cut[:, 96:128].reshape(64, LANES), 1, 1)
    after = pltpu.roll(cut[:, 0:32].reshape(64, LANES), LANES - 1, 1)
    dst[row : row + 2, 0:32, :] = before.astype(bf16).reshape(2, 32, LANES)
    dst[row : row + 2, 160:192, :] = after.astype(bf16).reshape(2, 32, LANES)


def set_lift(x0, rows):
    for pair in range(len(rows) // 2):
        both = jnp.concatenate([widened(rows[2 * pair]), widened(rows[2 * pair + 1])], axis=0)
        x0[16 * pair : 16 * pair + 16, :] = both.astype(bf16)


def lift(x0, dst, weight, out_rows, finish):
    for start, size in groups_of(out_rows // 2):
        x = jnp.concatenate([x0[16 * (start + g) : 16 * (start + g) + 32, :] for g in range(size)], axis=1)
        y = jnp.dot(weight, x, preferred_element_type=f32)
        for g in range(size):
            row = 2 * (start + g)
            put(dst, row, finish(y[:, g * LANES : (g + 1) * LANES], row))


def hidden(src, dst, weight, out_rows, finish):
    for start, size in groups_of(out_rows // 2):
        x = jnp.concatenate(
            [src[2 * (start + g) : 2 * (start + g) + 4].reshape(768, LANES) for g in range(size)], axis=1
        )
        y = jnp.dot(weight[...], x, preferred_element_type=f32)
        for g in range(size):
            row = 2 * (start + g)
            put(dst, row, finish(y[:, g * LANES : (g + 1) * LANES], row))


def project(src, weight, in_rows):
    parts = []
    for start, size in groups_of(in_rows // 2):
        x = jnp.concatenate(
            [src[2 * (start + g) : 2 * (start + g) + 2, 32:160, :].reshape(256, LANES) for g in range(size)], axis=1
        )
        y = jnp.dot(weight, x, preferred_element_type=f32)
        parts += [y[:, g * LANES : (g + 1) * LANES] for g in range(size)]
    rows = []
    for row in range(1, in_rows - 1):
        pair, odd = divmod(row, 2)
        if odd:
            total = parts[pair][16:24] + parts[pair + 1][0:8]
        else:
            total = parts[pair][8:16] + parts[pair - 1][24:32]
        rows.append(folded(total))
    return rows


def split3(x):
    hi = x.astype(bf16)
    rest = x - hi.astype(f32)
    mid = rest.astype(bf16)
    low = (rest - mid.astype(f32)).astype(bf16)
    return jnp.concatenate([hi, mid, low], axis=0)


def permuted(x, perm):
    rows = x.shape[0]
    y = jnp.dot(split3(x), perm, preferred_element_type=f32)
    return (y[:rows] + y[rows : 2 * rows]) + y[2 * rows :]


def split_perm(shift):
    x = lax.broadcasted_iota(jnp.int32, (COLS, COLS), 0)
    place = lax.broadcasted_iota(jnp.int32, (COLS, COLS), 1)
    column = 4 * (place & 127) + (place >> 7)
    return jnp.where(((x - column + shift) & 511) == 0, 1.0, 0.0).astype(bf16)


def join_perm(shift):
    place = lax.broadcasted_iota(jnp.int32, (COLS, COLS), 0)
    x = lax.broadcasted_iota(jnp.int32, (COLS, COLS), 1)
    column = 4 * (place & 127) + (place >> 7)
    return jnp.where(((x - column + shift) & 511) == 0, 1.0, 0.0).astype(bf16)


def store_split(dst, first, values):
    rows = values.shape[0]
    for s in range(4):
        dst[first : first + rows, 1 + s, :] = values[:, s * LANES : (s + 1) * LANES]


def joined(src, rows):
    return jnp.concatenate([src[0:rows, 1 + s, :] for s in range(4)], axis=1)


def kernel(
    shift_ref, force_ref, m2, m1, own, p1, p2, after, before, wide_ref, narrow_ref, out_ref,
    updated_ref, mismatch_ref,
    nat, field, target, prior, x0, wide, a1, a2, a3, b1, b2, b3, g1, g2, g3, fields,
):
    for layer in range(4):
        base = wide_ref[layer].astype(f32)
        for p in range(8):
            offset = 192 * (p // 4) + 32 * (p % 4)
            moved = base if offset == 0 else pltpu.roll(base, offset, 1)
            wide[layer, 32 * p : 32 * p + 32, :] = moved.astype(bf16)
    lifts = []
    for layer in range(2):
        base = narrow_ref[layer].astype(f32)
        made = []
        for p in range(8):
            offset = 8 * (p // 4) + p % 4
            moved = base if offset == 0 else pltpu.roll(base, offset, 1)
            made.append(moved[:, 0:32])
        lifts.append(jnp.concatenate(made, axis=0).astype(bf16))
    second, third, back_third, back_second = (wide.at[i] for i in range(4))
    w_out, w_back_out = out_ref[0], out_ref[1]

    nat[0:8, :] = m2[...]
    nat[8:16, :] = m1[...]
    nat[16:24, :] = own[...]
    nat[24:32, :] = p1[...]
    nat[32:40, :] = p2[...]
    nat[40:64, :] = before[0:24, :]
    store_split(field, 0, permuted(nat[...], split_perm(0)))
    store_split(target, 0, permuted(after[...], split_perm(shift_ref[0])))

    def tanh_of(y, row):
        return jnp.tanh(y)

    def advance(rows, h1, h2, h3, first):
        count = len(rows)
        set_lift(x0, rows)
        lift(x0, h1, lifts[0], count - 2, tanh_of)
        hidden(h1, h2, second, count - 4, tanh_of)
        hidden(h2, h3, third, count - 6, tanh_of)
        pushed = project(h3, w_out, count - 6)
        return [
            w + time_step * (t + force_ref[first + r] - drag_rate * w)
            for r, (w, t) in enumerate(zip(rows[4:-4], pushed))
        ]

    def masked_by(h, offset):
        def finish(y, row):
            value = h[row + offset : row + offset + 2, 32:160, :].astype(f32).reshape(256, LANES)
            return y * (1.0 - value * value)

        return finish

    def retreat(rows, h1, h2, h3, offset):
        count = len(rows)
        set_lift(x0, [time_step * l for l in rows])
        lift(x0, g3, lifts[1], count - 2, masked_by(h3, offset))
        hidden(g3, g2, back_third, count - 4, masked_by(h2, offset + 2))
        hidden(g2, g1, back_second, count - 6, masked_by(h1, offset + 4))
        pulled = project(g1, w_back_out, count - 6)
        return [l * (1.0 - time_step * drag_rate) + t for l, t in zip(rows[4:-4], pulled)]

    start = [field[r] for r in range(40)]
    middle = advance(start, a1, a2, a3, 0)
    end = advance(middle, b1, b2, b3, 4)
    gap = [e - target[r] for r, e in enumerate(end)]
    for r in range(8):
        fields[r] = gap[8 + r]
    adjoint = retreat(gap, b1, b2, b3, 2)
    adjoint = retreat(adjoint, a1, a2, a3, 10)
    for r in range(8):
        fields[8 + r] = adjoint[r]

    preceding = [field[40 + r] for r in range(24)]
    preceding = advance(preceding, g1, g2, g3, 8)
    preceding = advance(preceding, g1, g2, g3, 12)
    for r in range(8):
        prior[r] = preceding[r]

    both = permuted(joined(fields, 16), join_perm(0))
    mismatch_ref[...] = both[0:8]
    shift_before = before[24:25, :].astype(jnp.int32)
    back = permuted(joined(prior, 8), join_perm(shift_before)) - own[...]
    updated_ref[...] = own[...] - learn_rate * (both[8:16] - back)


def hidden_base(kernel_taps):
    taps = jnp.transpose(kernel_taps, (3, 0, 1, 2)).reshape(32, 3, 96)
    return jnp.pad(taps, ((0, 0), (0, 1), (0, 96))).reshape(32, 768)


def lift_base(taps):
    taps = jnp.pad(jnp.transpose(taps, (2, 0, 1)), ((0, 0), (0, 0), (0, 5))).reshape(32, 24)
    return jnp.pad(taps, ((0, 0), (0, 104)))


def out_weight(taps):
    padded = jnp.pad(taps, ((1, 1), (3, 3), (0, 0)))
    rows = []
    for row in range(4):
        for slot in range(8):
            if slot < 6:
                rows.append(padded[3 - row : 5 - row, 5 - slot : 9 - slot, :].reshape(256))
            else:
                rows.append(jnp.zeros((256,), taps.dtype))
    return jnp.stack(rows)


def reverse_kernel(kernel_taps):
    return jnp.transpose(kernel_taps[::-1, ::-1], (0, 1, 3, 2))


def per_device(initial_states, w_lift, w_second, w_third, w_project, shift_cells, wavenumber):
    segs, strips = lax.axis_size("seg"), lax.axis_size("space")
    total_rows = ROWS * strips
    own = initial_states[0]

    def fetch(x, by_seg, by_strip):
        pairs = []
        for s in range(segs):
            for p in range(strips):
                pairs.append((((s + by_seg) % segs) * strips + (p + by_strip) % strips, s * strips + p))
        return lax.ppermute(x, ("seg", "space"), pairs)

    m2, m1, p1, p2 = (fetch(own, 0, by) for by in (-2, -1, 1, 2))
    middle = jnp.concatenate([m1, own, p1], axis=0)
    shift_row = jnp.broadcast_to(shift_cells.astype(f32)[:, None], (8, COLS))
    after = fetch(middle, 1, 0)
    before = fetch(jnp.concatenate([middle, shift_row], axis=0), -1, 0)

    row_ids = lax.axis_index("space") * ROWS + jnp.arange(32, dtype=jnp.int32) - 12
    row_ids = (row_ids + total_rows) % total_rows
    phase_first = (wavenumber[0] * row_ids % total_rows).astype(f32)
    phase_second = (wavenumber[1] * row_ids % total_rows).astype(f32)
    forcing = jnp.cos(2.0 * math.pi * phase_first / total_rows) + 0.5 * jnp.sin(
        2.0 * math.pi * phase_second / total_rows
    )
    wide = jnp.stack(
        [hidden_base(w_second), hidden_base(w_third), hidden_base(reverse_kernel(w_third)), hidden_base(reverse_kernel(w_second))]
    )
    narrow = jnp.stack([lift_base(w_lift[:, :, 0, :]), lift_base(w_project[::-1, ::-1, :, 0])])
    out = jnp.stack([out_weight(w_project[:, :, :, 0]), out_weight(w_lift[::-1, ::-1, 0, :])])

    vmem = pl.BlockSpec(memory_space=pltpu.VMEM)
    smem = pl.BlockSpec(memory_space=pltpu.SMEM)

    def hid(rows):
        return pltpu.VMEM((rows, 192, LANES), bf16)

    def fld(rows):
        return pltpu.VMEM((rows, 8, LANES), f32)

    updated, mismatch = pl.pallas_call(
        kernel,
        out_shape=[jax.ShapeDtypeStruct((ROWS, COLS), f32)] * 2,
        in_specs=[smem, smem] + [vmem] * 10,
        out_specs=[vmem, vmem],
        scratch_shapes=[
            pltpu.VMEM((64, COLS), f32), fld(64), fld(24), fld(8), pltpu.VMEM((320, LANES), bf16),
            pltpu.VMEM((4, 256, 768), bf16),
            hid(38), hid(36), hid(34), hid(30), hid(28), hid(26), hid(22), hid(22), hid(22), fld(16),
        ],
        compiler_params=pltpu.CompilerParams(vmem_limit_bytes=48 * 1024 * 1024),
    )(shift_cells, forcing, m2, m1, own, p1, p2, after, before, wide, narrow, out)
    return updated[None], mismatch[None]


def solution(mesh):
    in_specs = (P("seg", "space", None), P(), P(), P(), P(), P("seg"), P())
    out_specs = (P("seg", "space", None), P("seg", "space", None))
    return jax.shard_map(per_device, mesh=mesh, in_specs=in_specs, out_specs=out_specs, check_vma=False)
```

profile of v0, /device:TPU:0, one launch (start us, length us, event | category | flops | bytes accessed | tf_op | source)
XLA Modules:
  0.0 44.9 jit_solution(4767124016014178050)
XLA Ops:
  0.6 0.1 collective-permute-start
  0.7 0.1 collective-permute-start.1
  0.8 4.6 %collective-permute-start.2 = (f32[8,512]{1,0:T(8,128)}, f32[8,512]{1,0:T(8,128)S(1)}, u32[]{:S(2)}, u32[]{:S(2)}) collective-permute-start(f32[8,512]{1,0:T(8,128)} %bitcast.37), channel_id=1, source_target_pairs={{1,0},{2,1},{3,2},{4,3},{5,4},{6,5},{7,6},{8,7},{9,8},{10,9},{11,1... | collective-permute-start | bytes 49160 | tf_op jit(solution)/shard_map/ppermute | solution.py:267
  5.5 2.2 %collective-permute-start.3 = (f32[8,512]{1,0:T(8,128)}, f32[8,512]{1,0:T(8,128)S(1)}, u32[]{:S(2)}, u32[]{:S(2)}) collective-permute-start(f32[8,512]{1,0:T(8,128)} %bitcast.38), channel_id=1, source_target_pairs={{2,0},{3,1},{4,2},{5,3},{6,4},{7,5},{8,6},{9,7},{10,8},{11,9},{12,... | collective-permute-start | bytes 49160 | tf_op jit(solution)/shard_map/ppermute | solution.py:267
  7.7 0.7 %rev.15 = bf16[3,3,1,32]{3,1,2,0:T(4,128)(2,1)S(1)} reverse(bf16[3,3,1,32]{3,1,2,0:T(4,128)(2,1)} %param.8), dimensions={0,1} | reverse | bytes 1152 | tf_op jit(solution)/shard_map/rev | solution.py:286
  8.5 0.9 %pad_slice_fusion.25 = (bf16[2,4,32]{2,1,0:T(4,128)(2,1)S(1)}, bf16[2,4,32]{2,1,0:T(4,128)(2,1)S(1)}, bf16[2,4,32]{2,1,0:T(4,128)(2,1)S(1)}, bf16[2,4,32]{2,1,0:T(4,128)(2,1)S(1)}, bf16[2,4,32]{2,1,0:T(4,128)(2,1)S(1)}) fusion(bf16[3,3,32]{2,1,0:T(4,128)(2,1)} %bitcast.46), kind=kLoop, calls=%fused_computation.26 | loop fusion | bytes 3136 | tf_op jit(solution)/shard_map/slice | solution.py:247
  9.4 0.1 reshape.30
  9.6 0.1 stack_reshape.159
  9.7 0.8 %copy-done.1 = bf16[3,3,32,32]{3,2,1,0:T(8,128)(2,1)S(1)} copy-done((bf16[3,3,32,32]{3,2,1,0:T(8,128)(2,1)S(1)}, bf16[3,3,32,32]{3,2,1,0:T(8,128)(2,1)}, u32[]{:S(2)}) %copy-start.1) | copy-done | bytes 18456
  10.5 0.1 reshape.29
  10.7 0.1 stack_reshape.158
  10.8 0.1 copy.14
  11.0 0.1 stack_reshape.157
  11.1 0.1 copy.13
  11.2 0.1 stack_reshape.156
  11.4 0.1 copy.21
  11.4 0.6 %copy-done.4 = bf16[3,3,1,32]{3,1,2,0:T(4,128)(2,1)S(1)} copy-done((bf16[3,3,1,32]{3,1,2,0:T(4,128)(2,1)S(1)}, bf16[3,3,1,32]{3,1,2,0:T(4,128)(2,1)}, u32[]{:S(2)}) %copy-start.4) | copy-done | bytes 600
  12.0 0.1 copy.19
  12.1 0.1 stack_reshape.184
  12.5 0.1 stack_reshape.188
  15.9 0.1 stack_reshape.181
  16.0 0.1 stack_reshape.182
  16.1 0.1 stack_reshape.183
  16.3 0.1 stack.33
  16.4 0.1 stack.31
  16.6 0.6 %copy-done.5 = s32[2]{0:T(128)S(1)} copy-done((s32[2]{0:T(128)S(1)}, s32[2]{0:T(128)}, u32[]{:S(2)}) %copy-start.5) | copy-done | bytes 32
  17.2 0.6 %fusion.11 = (s32[1]{0:T(128)}, s32[1]{0:T(128)}) fusion(s32[2]{0:T(128)S(1)} %copy-done.5), kind=kLoop, calls=%fused_computation.79 | loop fusion | bytes 16 | tf_op jit(solution)/shard_map/slice | solution.py:277
  18.6 5.2 %collective-permute-start.4 = (f32[24,512]{1,0:T(8,128)S(1)}, f32[24,512]{1,0:T(8,128)S(1)}, u32[]{:S(2)}, u32[]{:S(2)}) collective-permute-start(f32[24,512]{1,0:T(8,128)S(1)} %pad_maximum_fusion.1), channel_id=1, source_target_pairs={{32,0},{33,1},{34,2},{35,3},{36,4},{37,5},{38,6},{39,7},{40,8},{41... | collective-permute-start | bytes 147464 | tf_op jit(solution)/shard_map/ppermute | solution.py:267
  23.8 0.2 collective-permute-start.5
  24.0 1.4 %fusion.3.force_ref = f32[32]{0:T(128)S(1)} fusion(s32[]{:T(128)} %bitcast.1, s32[]{:T(128)S(6)} %mul.24, s32[]{:T(128)} %bitcast), kind=kLoop, calls=%fused_computation.71 | loop fusion | flops 1376 | bytes 140 | tf_op jit(solution)/shard_map/add | solution.py:279
  25.5 6.4 %collective-permute-done.5.before = f32[32,512]{1,0:T(8,128)S(1)} collective-permute-done((f32[32,512]{1,0:T(8,128)S(1)}, f32[32,512]{1,0:T(8,128)S(1)}, u32[]{:S(2)}, u32[]{:S(2)}) %collective-permute-start.5) | collective-permute-done | bytes 65568 | tf_op jit(solution)/shard_map/ppermute | solution.py:267
  31.9 13.0 %shard_map.86 = (f32[8,512]{1,0:T(8,128)}, f32[8,512]{1,0:T(8,128)}) custom-call(s32[1]{0:T(128)S(6)} %copy.28.shift_ref, f32[32]{0:T(128)S(1)} %fusion.3.force_ref, f32[8,512]{1,0:T(8,128)S(1)} %collective-permute-done.m2, f32[8,512]{1,0:T(8,128)S(1)} %collective-permute-done.1.m1, f32[8,512]{1,0:T(8,128)S(1)} %bitcast.41, ...), custom_call_target="tpu_custom_call" | custom-call | tf_op jit(solution)/shard_map/pallas_call | solution.py:297
  (80 shorter events, 4.3 us)
Async XLA Ops:
  0.6 8.7 %copy-start.2 = (bf16[3,3,32,32]{3,2,1,0:T(8,128)(2,1)S(1)}, bf16[3,3,32,32]{3,2,1,0:T(8,128)(2,1)}, u32[]{:S(2)}) copy-start(bf16[3,3,32,32]{3,2,1,0:T(8,128)(2,1)} %param.9) | copy-start | bytes 55300
  0.6 24.7 %collective-permute-start = (f32[8,512]{1,0:T(8,128)}, f32[8,512]{1,0:T(8,128)S(1)}, u32[]{:S(2)}, u32[]{:S(2)}) collective-permute-start(f32[8,512]{1,0:T(8,128)} %bitcast.35), channel_id=1, source_target_pairs={{30,0},{31,1},{0,2},{1,3},{2,4},{3,5},{4,6},{5,7},{6,8},{7,9},{8,1... | collective-permute-start | bytes 49160 | tf_op jit(solution)/shard_map/ppermute | solution.py:267
  0.7 17.8 %collective-permute-start.1 = (f32[8,512]{1,0:T(8,128)}, f32[8,512]{1,0:T(8,128)S(1)}, u32[]{:S(2)}, u32[]{:S(2)}) collective-permute-start(f32[8,512]{1,0:T(8,128)} %bitcast.36), channel_id=1, source_target_pairs={{31,0},{0,1},{1,2},{2,3},{3,4},{4,5},{5,6},{6,7},{7,8},{8,9},{9,10... | collective-permute-start | bytes 49160 | tf_op jit(solution)/shard_map/ppermute | solution.py:267
  0.8 17.7 %collective-permute-start.2 = (f32[8,512]{1,0:T(8,128)}, f32[8,512]{1,0:T(8,128)S(1)}, u32[]{:S(2)}, u32[]{:S(2)}) collective-permute-start(f32[8,512]{1,0:T(8,128)} %bitcast.37), channel_id=1, source_target_pairs={{1,0},{2,1},{3,2},{4,3},{5,4},{6,5},{7,6},{8,7},{9,8},{10,9},{11,1... | collective-permute-start | bytes 49160 | tf_op jit(solution)/shard_map/ppermute | solution.py:267
  5.5 19.9 %collective-permute-start.3 = (f32[8,512]{1,0:T(8,128)}, f32[8,512]{1,0:T(8,128)S(1)}, u32[]{:S(2)}, u32[]{:S(2)}) collective-permute-start(f32[8,512]{1,0:T(8,128)} %bitcast.38), channel_id=1, source_target_pairs={{2,0},{3,1},{4,2},{5,3},{6,4},{7,5},{8,6},{9,7},{10,8},{11,9},{12,... | collective-permute-start | bytes 49160 | tf_op jit(solution)/shard_map/ppermute | solution.py:267
  8.4 0.9 %copy-start.3 = (bf16[3,3,32,1]{2,1,3,0:T(4,128)(2,1)S(1)}, bf16[3,3,32,1]{2,1,3,0:T(4,128)(2,1)}, u32[]{:S(2)}) copy-start(bf16[3,3,32,1]{2,1,3,0:T(4,128)(2,1)} %param.11) | copy-start | bytes 1732
  9.6 0.9 %copy-start.1 = (bf16[3,3,32,32]{3,2,1,0:T(8,128)(2,1)S(1)}, bf16[3,3,32,32]{3,2,1,0:T(8,128)(2,1)}, u32[]{:S(2)}) copy-start(bf16[3,3,32,32]{3,2,1,0:T(8,128)(2,1)} %param.10) | copy-start | bytes 55300
  11.3 0.7 %copy-start.4 = (bf16[3,3,1,32]{3,1,2,0:T(4,128)(2,1)S(1)}, bf16[3,3,1,32]{3,1,2,0:T(4,128)(2,1)}, u32[]{:S(2)}) copy-start(bf16[3,3,1,32]{3,1,2,0:T(4,128)(2,1)} %param.8) | copy-start | bytes 1732
  16.5 0.7 %copy-start.5 = (s32[2]{0:T(128)S(1)}, s32[2]{0:T(128)}, u32[]{:S(2)}) copy-start(s32[2]{0:T(128)} %param.13) | copy-start | bytes 28
  17.2 1.3 %copy-start = (f32[1,8,512]{2,1,0:T(8,128)S(1)}, f32[1,8,512]{2,1,0:T(8,128)}, u32[]{:S(2)}) copy-start(f32[1,8,512]{2,1,0:T(8,128)} %param.7) | copy-start | bytes 49156
  18.6 6.9 %collective-permute-start.4 = (f32[24,512]{1,0:T(8,128)S(1)}, f32[24,512]{1,0:T(8,128)S(1)}, u32[]{:S(2)}, u32[]{:S(2)}) collective-permute-start(f32[24,512]{1,0:T(8,128)S(1)} %pad_maximum_fusion.1), channel_id=1, source_target_pairs={{32,0},{33,1},{34,2},{35,3},{36,4},{37,5},{38,6},{39,7},{40,8},{41... | collective-permute-start | bytes 147464 | tf_op jit(solution)/shard_map/ppermute | solution.py:267
  23.8 8.1 %collective-permute-start.5 = (f32[32,512]{1,0:T(8,128)S(1)}, f32[32,512]{1,0:T(8,128)S(1)}, u32[]{:S(2)}, u32[]{:S(2)}) collective-permute-start(f32[32,512]{1,0:T(8,128)S(1)} %maximum_maximum_fusion), channel_id=1, source_target_pairs={{224,0},{225,1},{226,2},{227,3},{228,4},{229,5},{230,6},{231,7},{2... | collective-permute-start | bytes 196616 | tf_op jit(solution)/shard_map/ppermute | solution.py:267
where the time goes:
time: 45.2 us; the launch traced here: 44.9 us
  Pallas kernels  13 us (29%)
  starting transfers between devices  12.4 us (27%)
  local copies, waits for them, and re-layouts  9.93 us (22%)
  waiting for transfers between devices  6.49 us (14%)
  between operations  1.57 us (3%)
  other arithmetic  1.48 us (3%)
    pallas_call x1, Pallas kernels, per_device(): pl.pallas_call(kernel, out_shape=[jax.ShapeDtypeStruct((ROWS, COLS), f32)...  13 us
    ppermute x6, starting transfers between devices, fetch(): return lax.ppermute(x, ('seg', 'space'), pairs)  12.4 us
    ppermute x6, waiting for transfers between devices, fetch(): return lax.ppermute(x, ('seg', 'space'), pairs)  6.49 us
    another operation x50, local copies, waits for them, and re-layouts, out_weight(): return jnp.stack(rows)  4.28 us
    unnamed x16, local copies, waits for them, and re-layouts  2.32 us
    add x1, other arithmetic, per_device(): jnp.cos(2.0 * math.pi * phase_first / total_rows)  1.36 us
    slice x4, local copies, waits for them, and re-layouts, out_weight(): rows.append(padded[3 - row:5 - row, 5 - slot:9 - slot, :].reshape(256))  0.92 us
  transfers between devices with their start and end apart: 6, of which 2 were waited for; matrix products, arithmetic and copies ran while one was open for 21% of the time, Pallas kernels for 0%

commit v1 on v0

v1 whole, which is shorter than its diff:
```python
import functools
import math

import jax
import jax.numpy as jnp
from jax import lax
from jax.experimental import pallas as pl
from jax.experimental.pallas import tpu as pltpu
from jax.sharding import PartitionSpec as P


time_step = 0.4
drag_rate = 0.1
learn_rate = 0.5

ROWS = 8
LANES = 128
COLS = 512
NY = 256
f32 = jnp.float32
bf16 = jnp.bfloat16


def groups_of(count, most=4):
    start = 0
    while start < count:
        size = min(most, count - start)
        yield start, size
        start += size


def slot_iota(shape):
    return lax.broadcasted_iota(jnp.int32, shape, len(shape) - 2)


def widened(field):
    slot = slot_iota(field.shape)
    moved = pltpu.roll(field, 4, 0)
    left = pltpu.roll(moved, 1, 1)
    right = pltpu.roll(moved, LANES - 1, 1)
    zero = jnp.zeros_like(field)
    return jnp.where((slot >= 1) & (slot <= 4), field, jnp.where(slot == 0, left, jnp.where(slot == 5, right, zero)))


def folded(partial):
    slot = slot_iota(partial.shape)
    moved = pltpu.roll(partial, 4, 0)
    left = pltpu.roll(moved, LANES - 1, 1)
    right = pltpu.roll(moved, 1, 1)
    return partial + jnp.where(slot == 4, left, jnp.where(slot == 1, right, jnp.zeros_like(partial)))


def put(dst, row, values):
    cut = values.reshape(2, 4 * 32, LANES)
    dst[row : row + 2, 32:160, :] = cut.astype(bf16)
    before = pltpu.roll(cut[:, 96:128].reshape(64, LANES), 1, 1)
    after = pltpu.roll(cut[:, 0:32].reshape(64, LANES), LANES - 1, 1)
    dst[row : row + 2, 0:32, :] = before.astype(bf16).reshape(2, 32, LANES)
    dst[row : row + 2, 160:192, :] = after.astype(bf16).reshape(2, 32, LANES)


def set_lift(x0, rows):
    for pair in range(len(rows) // 2):
        both = jnp.concatenate([widened(rows[2 * pair]), widened(rows[2 * pair + 1])], axis=0)
        x0[16 * pair : 16 * pair + 16, :] = both.astype(bf16)


def lift(x0, dst, weight, out_rows, finish):
    for start, size in groups_of(out_rows // 2):
        x = jnp.concatenate([x0[16 * (start + g) : 16 * (start + g) + 32, :] for g in range(size)], axis=1)
        y = jnp.dot(weight, x, preferred_element_type=f32)
        for g in range(size):
            row = 2 * (start + g)
            put(dst, row, finish(y[:, g * LANES : (g + 1) * LANES], row))


def hidden(src, dst, weight, out_rows, finish):
    for start, size in groups_of(out_rows // 2):
        x = jnp.concatenate(
            [src[2 * (start + g) : 2 * (start + g) + 4].reshape(768, LANES) for g in range(size)], axis=1
        )
        y = jnp.dot(weight[...], x, preferred_element_type=f32)
        for g in range(size):
            row = 2 * (start + g)
            put(dst, row, finish(y[:, g * LANES : (g + 1) * LANES], row))


def project(src, weight, in_rows):
    parts = []
    for start, size in groups_of(in_rows // 2):
        x = jnp.concatenate(
            [src[2 * (start + g) : 2 * (start + g) + 2, 32:160, :].reshape(256, LANES) for g in range(size)], axis=1
        )
        y = jnp.dot(weight, x, preferred_element_type=f32)
        parts += [y[:, g * LANES : (g + 1) * LANES] for g in range(size)]
    rows = []
    for row in range(1, in_rows - 1):
        pair, odd = divmod(row, 2)
        if odd:
            total = parts[pair][16:24] + parts[pair + 1][0:8]
        else:
            total = parts[pair][8:16] + parts[pair - 1][24:32]
        rows.append(folded(total))
    return rows


def split3(x):
    hi = x.astype(bf16)
    rest = x - hi.astype(f32)
    mid = rest.astype(bf16)
    low = (rest - mid.astype(f32)).astype(bf16)
    return jnp.concatenate([hi, mid, low], axis=0)


def permuted(x, perm):
    rows = x.shape[0]
    y = jnp.dot(split3(x), perm, preferred_element_type=f32)
    return (y[:rows] + y[rows : 2 * rows]) + y[2 * rows :]


def split_perm(shift):
    x = lax.broadcasted_iota(jnp.int32, (COLS, COLS), 0)
    place = lax.broadcasted_iota(jnp.int32, (COLS, COLS), 1)
    column = 4 * (place & 127) + (place >> 7)
    return jnp.where(((x - column + shift) & 511) == 0, 1.0, 0.0).astype(bf16)


def join_perm(shift):
    place = lax.broadcasted_iota(jnp.int32, (COLS, COLS), 0)
    x = lax.broadcasted_iota(jnp.int32, (COLS, COLS), 1)
    column = 4 * (place & 127) + (place >> 7)
    return jnp.where(((x - column + shift) & 511) == 0, 1.0, 0.0).astype(bf16)


def store_split(dst, first, values):
    rows = values.shape[0]
    for s in range(4):
        dst[first : first + rows, 1 + s, :] = values[:, s * LANES : (s + 1) * LANES]


def joined(src, rows):
    return jnp.concatenate([src[0:rows, 1 + s, :] for s in range(4)], axis=1)


def hidden_weight(base, dst, layer):
    for p in range(8):
        offset = 192 * (p // 4) + 32 * (p % 4)
        moved = base if offset == 0 else pltpu.roll(base, offset, 1)
        dst[layer, 32 * p : 32 * p + 32, :] = moved.astype(bf16)


def placed(blocks):
    gap = jnp.zeros((32, 96), f32)
    parts = []
    for a in range(3):
        parts += [blocks[3 * a], blocks[3 * a + 1], blocks[3 * a + 2], gap]
    return jnp.concatenate(parts + [gap, gap], axis=1)


def chosen(taps, index, flip):
    total = jnp.where(index == (8 if flip else 0), taps[0], 0.0)
    for t in range(1, 9):
        total = jnp.where(index == (8 - t if flip else t), taps[t], total)
    return total


def tap_index(a, b):
    return jnp.where((a >= 0) & (a <= 2) & (b >= 0) & (b <= 2), 3 * a + b, -1)


def rows_and_columns(ref):
    values = ref[...].astype(f32)
    rows = [values[t // 3, t % 3 : t % 3 + 1, :] for t in range(9)]
    at = lax.broadcasted_iota(jnp.int32, (32, 32), 0)
    total = jnp.zeros((32, 32), f32)
    for t in range(9):
        total = jnp.where(at == t, jnp.broadcast_to(rows[t], (32, 32)), total)
    turned = total.T
    return rows, [turned[:, t : t + 1] for t in range(9)]


def weights_kernel(
    place, number_hbm, shift_hbm, lift_hbm, second_hbm, third_hbm, project_hbm, wide, narrow, out, force, split, join,
    split_next, join_next, number, shift, lift_ref, second, third, project_ref, sems,
):
    pairs = (
        (number_hbm, number), (shift_hbm, shift), (lift_hbm, lift_ref), (project_hbm, project_ref),
        (second_hbm, second), (third_hbm, third),
    )
    copies = [pltpu.make_async_copy(src, dst, sems.at[i]) for i, (src, dst) in enumerate(pairs)]
    for copy in copies:
        copy.start()
    split[...] = split_perm(0)
    join[...] = join_perm(0)
    for copy in copies:
        copy.wait()
    split_next[...] = split_perm(shift[0])
    join_next[...] = join_perm(shift[0])
    row = place[0] + lax.broadcasted_iota(jnp.int32, (32, LANES), 0)
    first = ((number[0] * row) & (NY - 1)).astype(f32)
    other = ((number[1] * row) & (NY - 1)).astype(f32)
    force[...] = jnp.cos(2.0 * math.pi * first / NY) + 0.5 * jnp.sin(2.0 * math.pi * other / NY)
    for layer, taps in ((0, second), (1, third)):
        hidden_weight(placed([taps[t // 3, t % 3].astype(f32).T for t in range(9)]), wide, layer)
    for layer, taps in ((2, third), (3, second)):
        hidden_weight(placed([taps[2 - t // 3, 2 - t % 3].astype(f32) for t in range(9)]), wide, layer)

    lift_rows, lift_cols = rows_and_columns(lift_ref)
    project_rows, project_cols = rows_and_columns(project_ref)
    for layer, cols, flip in ((0, lift_cols, False), (1, project_cols, True)):
        lane = lax.broadcasted_iota(jnp.int32, (32, LANES), 1)
        taps = [jnp.broadcast_to(col, (32, LANES)) for col in cols]
        for p in range(8):
            index = jnp.where(lane < 32, tap_index((lane >> 3) - p // 4, (lane & 7) - p % 4), -1)
            narrow[layer, 32 * p : 32 * p + 32, :] = chosen(taps, index, flip).astype(bf16)

    row = lax.broadcasted_iota(jnp.int32, (32, 256), 0)
    lane = lax.broadcasted_iota(jnp.int32, (32, 256), 1)
    index = jnp.where((row & 7) < 6, tap_index((lane >> 7) - (row >> 3) + 2, ((lane >> 5) & 3) - (row & 7) + 2), -1)
    for layer, rows, flip in ((0, project_rows, False), (1, lift_rows, True)):
        taps = [jnp.broadcast_to(jnp.concatenate([r] * 8, axis=1), (32, 256)) for r in rows]
        out[layer] = chosen(taps, index, flip).astype(bf16)


def tanh_of(y, row):
    return jnp.tanh(y)


def advance(rows, x0, h1, h2, h3, weights, force, first):
    count = len(rows)
    wide, narrow, out = weights
    set_lift(x0, rows)
    lift(x0, h1, narrow[0, :, 0:32], count - 2, tanh_of)
    hidden(h1, h2, wide.at[0], count - 4, tanh_of)
    hidden(h2, h3, wide.at[1], count - 6, tanh_of)
    pushed = project(h3, out[0], count - 6)
    return [
        w + time_step * (t + force[first + r : first + r + 1, :] - drag_rate * w)
        for r, (w, t) in enumerate(zip(rows[4:-4], pushed))
    ]


def masked_by(h, offset):
    def finish(y, row):
        value = h[row + offset : row + offset + 2, 32:160, :].astype(f32).reshape(256, LANES)
        return y * (1.0 - value * value)

    return finish


def retreat(rows, x0, history, made, weights, offset):
    count = len(rows)
    wide, narrow, out = weights
    (h1, h2, h3), (g1, g2, g3) = history, made
    set_lift(x0, [time_step * l for l in rows])
    lift(x0, g3, narrow[1, :, 0:32], count - 2, masked_by(h3, offset))
    hidden(g3, g2, wide.at[2], count - 4, masked_by(h2, offset + 2))
    hidden(g2, g1, wide.at[3], count - 6, masked_by(h1, offset + 4))
    pulled = project(g1, out[1], count - 6)
    return [l * (1.0 - time_step * drag_rate) + t for l, t in zip(rows[4:-4], pulled)]


def forward_kernel(m2, m1, own, p1, p2, wide, narrow, out, force, split, end, a1, a2, a3, b1, b2, b3, nat, field, x0):
    nat[0:8, :] = m2[...]
    nat[8:16, :] = m1[...]
    nat[16:24, :] = own[...]
    nat[24:32, :] = p1[...]
    nat[32:40, :] = p2[...]
    store_split(field, 0, permuted(nat[...], split[...]))
    weights = (wide, narrow, out)
    middle = advance([field[r] for r in range(40)], x0, a1, a2, a3, weights, force, 0)
    for r, row in enumerate(advance(middle, x0, b1, b2, b3, weights, force, 4)):
        end[r] = row


def gap_kernel(end, after, split_next, join_next, gap, back, target, fields):
    store_split(target, 0, permuted(after[...], split_next[...]))
    for r in range(24):
        gap[r] = end[r] - target[r]
    for r in range(8):
        fields[r] = gap[8 + r]
    back[...] = permuted(joined(fields, 8), join_next[...])


def adjoint_kernel(
    gap, a1, a2, a3, b1, b2, b3, wide, narrow, out, join, adjoint, mismatch, x0, g1, g2, g3, fields
):
    weights = (wide, narrow, out)
    rows = [gap[r] for r in range(24)]
    for r in range(8):
        fields[r] = rows[8 + r]
    rows = retreat(rows, x0, (b1, b2, b3), (g1, g2, g3), weights, 2)
    rows = retreat(rows, x0, (a1, a2, a3), (g1, g2, g3), weights, 10)
    for r in range(8):
        fields[8 + r] = rows[r]
    both = permuted(joined(fields, 16), join[...])
    mismatch[...] = both[0:8]
    adjoint[...] = both[8:16]


def per_device(initial_states, w_lift, w_second, w_third, w_project, shift_cells, wavenumber):
    segs, strips = lax.axis_size("seg"), lax.axis_size("space")
    total_rows = ROWS * strips
    own = initial_states[0]

    def fetch(x, by_seg, by_strip):
        pairs = []
        for s in range(segs):
            for p in range(strips):
                pairs.append((((s + by_seg) % segs) * strips + (p + by_strip) % strips, s * strips + p))
        return lax.ppermute(x, ("seg", "space"), pairs)

    m2, m1, p1, p2 = (fetch(own, 0, by) for by in (-2, -1, 1, 2))
    after = fetch(jnp.concatenate([m1, own, p1], axis=0), 1, 0)

    vmem = pl.BlockSpec(memory_space=pltpu.VMEM)
    smem = pl.BlockSpec(memory_space=pltpu.SMEM)

    def hid(rows):
        return pltpu.VMEM((rows, 192, LANES), bf16)

    def fld(rows):
        return pltpu.VMEM((rows, 8, LANES), f32)

    def params(mib):
        return pltpu.CompilerParams(vmem_limit_bytes=mib * 1024 * 1024)

    def cost(us):
        return pl.CostEstimate(flops=int(us * 1000000000), bytes_accessed=1000, transcendentals=0)

    nat = jax.ShapeDtypeStruct((ROWS, COLS), f32)
    x0 = pltpu.VMEM((320, LANES), bf16)
    place = lax.axis_index("space") * ROWS + total_rows - 12
    hbm = pl.BlockSpec(memory_space=pl.ANY)
    perm = pltpu.VMEM((COLS, COLS), bf16)
    wide, narrow, out, force, split, join, split_next, join_next = pl.pallas_call(
        weights_kernel,
        out_shape=[
            pltpu.VMEM((4, 256, 768), bf16), pltpu.VMEM((2, 256, LANES), bf16), pltpu.VMEM((2, 32, 256), bf16),
            pltpu.VMEM((32, LANES), f32), perm, perm, perm, perm,
        ],
        in_specs=[smem] + [hbm] * 6,
        out_specs=[vmem] * 8,
        scratch_shapes=[
            pltpu.SMEM((2,), jnp.int32), pltpu.SMEM((1,), jnp.int32), pltpu.VMEM((3, 3, 32), bf16),
            pltpu.VMEM((3, 3, 32, 32), bf16), pltpu.VMEM((3, 3, 32, 32), bf16), pltpu.VMEM((3, 3, 32), bf16),
            pltpu.SemaphoreType.DMA((6,)),
        ],
        cost_estimate=cost(2),
        compiler_params=params(56),
    )(place.astype(jnp.int32)[None], wavenumber, shift_cells, w_lift.reshape(3, 3, 32), w_second, w_third, w_project.reshape(3, 3, 32))

    end, *history = pl.pallas_call(
        forward_kernel,
        out_shape=[fld(24), hid(38), hid(36), hid(34), hid(30), hid(28), hid(26)],
        in_specs=[vmem] * 10,
        out_specs=[vmem] * 7,
        scratch_shapes=[pltpu.VMEM((40, COLS), f32), fld(40), x0],
        cost_estimate=cost(6),
        compiler_params=params(8),
    )(m2, m1, own, p1, p2, wide, narrow, out, force, split)

    gap, back = pl.pallas_call(
        gap_kernel,
        out_shape=[fld(24), pltpu.VMEM((ROWS, COLS), f32)],
        in_specs=[vmem] * 4,
        out_specs=[vmem] * 2,
        scratch_shapes=[fld(24), fld(8)],
        cost_estimate=cost(1),
        compiler_params=params(8),
    )(end, after, split_next, join_next)
    preceding = fetch(back, -1, 0)

    adjoint, mismatch = pl.pallas_call(
        adjoint_kernel,
        out_shape=[pltpu.VMEM((ROWS, COLS), f32), nat],
        in_specs=[vmem] * 11,
        out_specs=[vmem] * 2,
        scratch_shapes=[x0, hid(22), hid(22), hid(22), fld(16)],
        cost_estimate=cost(4),
        compiler_params=params(12),
    )(gap, *history, wide, narrow, out, join)
    updated = own - learn_rate * (adjoint - preceding)
    return updated[None], mismatch[None]


def solution(mesh):
    in_specs = (P("seg", "space", None), P(), P(), P(), P(), P("seg"), P())
    out_specs = (P("seg", "space", None), P("seg", "space", None))
    return jax.shard_map(per_device, mesh=mesh, in_specs=in_specs, out_specs=out_specs, check_vma=False)
```

time: 45.2 us -> 31.6 us (0.70)
  local copies, waits for them, and re-layouts: 9.93 us -> 0.01 us
  waiting for transfers between devices: 6.49 us -> 3.22 us
  starting transfers between devices: 12.4 us -> 14.3 us
  Pallas kernels: 13 us -> 12 us
  other arithmetic: 1.48 us -> 0.62 us
    another operation x58 -> x0, local copies, waits for them, and re-layouts: 4.79 us -> none  [the longest x50 4.28 us: out_weight(): return jnp.stack(rows)]
    ppermute x6, waiting for transfers between devices: 6.49 us -> 3.22 us  [fetch(): return lax.ppermute(x, ('seg', 'space'), pairs)]
    unnamed x16 -> x2, local copies, waits for them, and re-layouts: 2.32 us -> 0.01 us
    ppermute x6, starting transfers between devices: 12.4 us -> 14.3 us  [fetch(): return lax.ppermute(x, ('seg', 'space'), pairs)]
    slice x5 -> x0, local copies, waits for them, and re-layouts: 1.5 us -> none  [the longest x4 0.92 us: out_weight(): rows.append(padded[3 - row:5 - row, 5 - slot:9 - slot, :].reshape(256))]
    add x1 -> x0, other arithmetic: 1.36 us -> none  [per_device(): jnp.cos(2.0 * math.pi * phase_first / total_rows)]
    pallas_call x1 -> x4, Pallas kernels: 13 us -> 12 us  [the longest x1 5.05 us: per_device(): pl.pallas_call(forward_kernel, out_shape=[fld(24), hid(38), hid(36), hid(...]
    rev x2 -> x0, local copies, waits for them, and re-layouts: 0.74 us -> none  [the longest x1 0.71 us: per_device(): w_lift[::-1, ::-1, 0, :]]
  transfers between devices with their start and end apart: 6 -> 6, of which waited for: 2 -> 1; matrix products, arithmetic and copies ran while one was open for 21% -> 0% of each run, Pallas kernels for 0% -> 37%
where the time goes in v1:
time: 31.6 us; the launch traced here: 31.5 us
  starting transfers between devices  14.3 us (45%)
  Pallas kernels  12 us (38%)
  waiting for transfers between devices  3.22 us (10%)
  between operations  1.36 us (4%)
  other arithmetic  0.62 us (2%)
    ppermute x6, starting transfers between devices, fetch(): return lax.ppermute(x, ('seg', 'space'), pairs)  14.3 us
    pallas_call x1, Pallas kernels, per_device(): pl.pallas_call(forward_kernel, out_shape=[fld(24), hid(38), hid(36), hid(...  5.05 us
    pallas_call x1, Pallas kernels, per_device(): pl.pallas_call(adjoint_kernel, out_shape=[pltpu.VMEM((ROWS, COLS), f32),...  4.13 us
    ppermute x6, waiting for transfers between devices, fetch(): return lax.ppermute(x, ('seg', 'space'), pairs)  3.22 us
    pallas_call x1, Pallas kernels, per_device(): pl.pallas_call(weights_kernel, out_shape=[pltpu.VMEM((4, 256, 768), bf16)...  2.44 us
  transfers between devices with their start and end apart: 6, of which 1 were waited for; matrix products, arithmetic and copies ran while one was open for 0% of the time, Pallas kernels for 37%

profile of v1, /device:TPU:0, one launch (start us, length us, event | category | flops | bytes accessed | tf_op | source)
XLA Modules:
  0.0 31.5 jit_solution(891044908167227313)
XLA Ops:
  0.6 0.1 collective-permute-start.1
  0.7 4.6 %collective-permute-start.2 = (f32[8,512]{1,0:T(8,128)}, f32[8,512]{1,0:T(8,128)S(1)}, u32[]{:S(2)}, u32[]{:S(2)}) collective-permute-start(f32[8,512]{1,0:T(8,128)} %bitcast.9), channel_id=1, source_target_pairs={{1,0},{2,1},{3,2},{4,3},{5,4},{6,5},{7,6},{8,7},{9,8},{10,9},{11,1... | collective-permute-start | bytes 49160 | tf_op jit(solution)/shard_map/ppermute | solution.py:311
  5.4 0.0 collective-permute-start
  5.4 4.1 %collective-permute-start.3 = (f32[8,512]{1,0:T(8,128)}, f32[8,512]{1,0:T(8,128)S(1)}, u32[]{:S(2)}, u32[]{:S(2)}) collective-permute-start(f32[8,512]{1,0:T(8,128)} %bitcast.11), channel_id=1, source_target_pairs={{2,0},{3,1},{4,2},{5,3},{6,4},{7,5},{8,6},{9,7},{10,8},{11,9},{12,... | collective-permute-start | bytes 49160 | tf_op jit(solution)/shard_map/ppermute | solution.py:311
  10.2 0.0 copy-start
  10.2 2.4 %shard_map.86 = (bf16[4,256,768]{2,1,0:T(8,128)(2,1)S(1)}, bf16[2,256,128]{2,1,0:T(8,128)(2,1)S(1)}, bf16[2,32,256]{2,1,0:T(8,128)(2,1)S(1)}, f32[32,128]{1,0:T(...) custom-call(s32[1]{0:T(128)} %bitcast.1.place, ...), custom_call_target="tpu_custom_call" | custom-call | flops 2000000000 | bytes 1000 | tf_op jit(solution)/shard_map/pallas_call | solution.py:336
  12.6 0.0 collective-permute-done.1.m1
  12.6 0.0 collective-permute-done.2.p1
  12.6 0.0 copy-done
  12.7 5.2 %collective-permute-start.4 = (f32[24,512]{1,0:T(8,128)S(1)}, f32[24,512]{1,0:T(8,128)S(1)}, u32[]{:S(2)}, u32[]{:S(2)}) collective-permute-start(f32[24,512]{1,0:T(8,128)S(1)} %pad_maximum_fusion), channel_id=1, source_target_pairs={{32,0},{33,1},{34,2},{35,3},{36,4},{37,5},{38,6},{39,7},{40,8},{41... | collective-permute-start | bytes 147464 | tf_op jit(solution)/shard_map/ppermute | solution.py:311
  17.8 0.0 collective-permute-done.m2
  17.8 0.0 collective-permute-done.3.p2
  17.8 5.1 %shard_map.87 = (f32[24,8,128]{2,1,0:T(8,128)S(1)}, bf16[38,192,128]{2,1,0:T(8,128)(2,1)S(1)}, bf16[36,192,128]{2,1,0:T(8,128)(2,1)S(1)}, bf16[34,192,128]{2,1,0...) custom-call(f32[8,512]{1,0:T(8,128)S(1)} %collective-permute-done.m2, ...), custom_call_target="tpu_custom_call" | custom-call | flops 6000000000 | bytes 1000 | tf_op jit(solution)/shard_map/pallas_call | solution.py:353
  22.9 0.0 collective-permute-done.4.after
  22.9 0.4 %shard_map.88 = (f32[24,8,128]{2,1,0:T(8,128)S(1)}, f32[8,512]{1,0:T(8,128)S(1)}) custom-call(f32[24,8,128]{2,1,0:T(8,128)S(1)} %get-tuple-element.26.end, f32[24,512]{1,0:T(8,128)S(1)} %collective-permute-done.4.after, bf16[512,512]{1,0:T(8,128)(2,1)S(1)} %get-tuple-element.27.split_next, bf16[512,512]{1,0:T(8,128)(2,1)S(1)} %get-tuple-element.28.join_next), custom_call_target="tpu_custom_call" | custom-call | flops 1000000000 | bytes 1000 | tf_op jit(solution)/shard_map/pallas_call | solution.py:363
  23.3 0.2 collective-permute-start.5
  23.5 4.1 %shard_map.89 = (f32[8,512]{1,0:T(8,128)S(1)}, f32[8,512]{1,0:T(8,128)}) custom-call(f32[24,8,128]{2,1,0:T(8,128)S(1)} %get-tuple-element.29.gap, bf16[38,192,128]{2,1,0:T(8,128)(2,1)S(1)} %get-tuple-element.30.a1, bf16[36,192,128]{2,1,0:T(8,128)(2,1)S(1)} %get-tuple-element.31.a2, bf16[34,192,128]{2,1,0:T(8,128)(2,1)S(1)} %get-tuple-element.32.a3, ...), custom_call_target="tpu_custom_call" | custom-call | flops 4000000000 | bytes 1000 | tf_op jit(solution)/shard_map/pallas_call | solution.py:374
  27.7 3.2 %collective-permute-done.5 = f32[8,512]{1,0:T(8,128)S(1)} collective-permute-done((f32[8,512]{1,0:T(8,128)S(1)}, f32[8,512]{1,0:T(8,128)S(1)}, u32[]{:S(2)}, u32[]{:S(2)}) %collective-permute-start.5) | collective-permute-done | bytes 16416 | tf_op jit(solution)/shard_map/ppermute | solution.py:311
  30.9 0.6 %subtract_bitcast_fusion = f32[1,8,512]{2,1,0:T(8,128)} fusion(f32[8,512]{1,0:T(8,128)S(1)} %get-tuple-element.37, f32[8,512]{1,0:T(8,128)S(1)} %collective-permute-done.5, f32[1,8,512]{2,1,0:T(8,128)S(1)} %copy-done), kind=kLoop, calls=%fused_computation.1 | loop fusion | flops 12288 | bytes 65536 | tf_op jit(solution)/shard_map/broadcast_in_dim | solution.py:384
  (1 shorter events, 0.0 us)
Async XLA Ops:
  0.6 12.0 %collective-permute-start.1 = (f32[8,512]{1,0:T(8,128)}, f32[8,512]{1,0:T(8,128)S(1)}, u32[]{:S(2)}, u32[]{:S(2)}) collective-permute-start(f32[8,512]{1,0:T(8,128)} %bitcast.8), channel_id=1, source_target_pairs={{31,0},{0,1},{1,2},{2,3},{3,4},{4,5},{5,6},{6,7},{7,8},{8,9},{9,10... | collective-permute-start | bytes 49160 | tf_op jit(solution)/shard_map/ppermute | solution.py:311
  0.7 11.9 %collective-permute-start.2 = (f32[8,512]{1,0:T(8,128)}, f32[8,512]{1,0:T(8,128)S(1)}, u32[]{:S(2)}, u32[]{:S(2)}) collective-permute-start(f32[8,512]{1,0:T(8,128)} %bitcast.9), channel_id=1, source_target_pairs={{1,0},{2,1},{3,2},{4,3},{5,4},{6,5},{7,6},{8,7},{9,8},{10,9},{11,1... | collective-permute-start | bytes 49160 | tf_op jit(solution)/shard_map/ppermute | solution.py:311
  5.4 12.5 %collective-permute-start = (f32[8,512]{1,0:T(8,128)}, f32[8,512]{1,0:T(8,128)S(1)}, u32[]{:S(2)}, u32[]{:S(2)}) collective-permute-start(f32[8,512]{1,0:T(8,128)} %bitcast.10), channel_id=1, source_target_pairs={{30,0},{31,1},{0,2},{1,3},{2,4},{3,5},{4,6},{5,7},{6,8},{7,9},{8,1... | collective-permute-start | bytes 49160 | tf_op jit(solution)/shard_map/ppermute | solution.py:311
  5.4 12.5 %collective-permute-start.3 = (f32[8,512]{1,0:T(8,128)}, f32[8,512]{1,0:T(8,128)S(1)}, u32[]{:S(2)}, u32[]{:S(2)}) collective-permute-start(f32[8,512]{1,0:T(8,128)} %bitcast.11), channel_id=1, source_target_pairs={{2,0},{3,1},{4,2},{5,3},{6,4},{7,5},{8,6},{9,7},{10,8},{11,9},{12,... | collective-permute-start | bytes 49160 | tf_op jit(solution)/shard_map/ppermute | solution.py:311
  10.2 2.5 %copy-start = (f32[1,8,512]{2,1,0:T(8,128)S(1)}, f32[1,8,512]{2,1,0:T(8,128)}, u32[]{:S(2)}) copy-start(f32[1,8,512]{2,1,0:T(8,128)} %param.7) | copy-start | bytes 49156
  12.7 10.2 %collective-permute-start.4 = (f32[24,512]{1,0:T(8,128)S(1)}, f32[24,512]{1,0:T(8,128)S(1)}, u32[]{:S(2)}, u32[]{:S(2)}) collective-permute-start(f32[24,512]{1,0:T(8,128)S(1)} %pad_maximum_fusion), channel_id=1, source_target_pairs={{32,0},{33,1},{34,2},{35,3},{36,4},{37,5},{38,6},{39,7},{40,8},{41... | collective-permute-start | bytes 147464 | tf_op jit(solution)/shard_map/ppermute | solution.py:311
  23.3 7.6 %collective-permute-start.5 = (f32[8,512]{1,0:T(8,128)S(1)}, f32[8,512]{1,0:T(8,128)S(1)}, u32[]{:S(2)}, u32[]{:S(2)}) collective-permute-start(f32[8,512]{1,0:T(8,128)S(1)} %get-tuple-element.38), channel_id=1, source_target_pairs={{224,0},{225,1},{226,2},{227,3},{228,4},{229,5},{230,6},{231,7},{2... | collective-permute-start | bytes 49160 | tf_op jit(solution)/shard_map/ppermute | solution.py:311

commit v2 on v1

--- a/solution.py
+++ b/solution.py
@@ -21,7 +21,7 @@
 bf16 = jnp.bfloat16
 
 
-def groups_of(count, most=4):
+def groups_of(count, most=2):
     start = 0
     while start < count:
         size = min(most, count - start)
@@ -180,7 +180,7 @@
 
 
 def weights_kernel(
-    place, number_hbm, shift_hbm, lift_hbm, second_hbm, third_hbm, project_hbm, wide, narrow, out, force, split, join,
+    code, number_hbm, shift_hbm, lift_hbm, second_hbm, third_hbm, project_hbm, wide, narrow, out, force, split, join,
     split_next, join_next, number, shift, lift_ref, second, third, project_ref, sems,
 ):
     pairs = (
@@ -196,7 +196,7 @@
         copy.wait()
     split_next[...] = split_perm(shift[0])
     join_next[...] = join_perm(shift[0])
-    row = place[0] + lax.broadcasted_iota(jnp.int32, (32, LANES), 0)
+    row = ROWS * (code[0] & 31) + NY - 12 + lax.broadcasted_iota(jnp.int32, (32, LANES), 0)
     first = ((number[0] * row) & (NY - 1)).astype(f32)
     other = ((number[1] * row) & (NY - 1)).astype(f32)
     force[...] = jnp.cos(2.0 * math.pi * first / NY) + 0.5 * jnp.sin(2.0 * math.pi * other / NY)
@@ -260,11 +260,19 @@
     return [l * (1.0 - time_step * drag_rate) + t for l, t in zip(rows[4:-4], pulled)]
 
 
-def forward_kernel(m2, m1, own, p1, p2, wide, narrow, out, force, split, end, a1, a2, a3, b1, b2, b3, nat, field, x0):
+def by_strip(code, within, across):
+    even = (code[0] & 1) == 0
+    return jnp.where(even, across, within), jnp.where(even, within, across)
+
+
+def forward_kernel(
+    code, m2, within, own, across, p2, wide, narrow, out, force, split, end, a1, a2, a3, b1, b2, b3, nat, field, x0
+):
+    m1, p1 = by_strip(code, within[...], across[...])
     nat[0:8, :] = m2[...]
-    nat[8:16, :] = m1[...]
+    nat[8:16, :] = m1
     nat[16:24, :] = own[...]
-    nat[24:32, :] = p1[...]
+    nat[24:32, :] = p1
     nat[32:40, :] = p2[...]
     store_split(field, 0, permuted(nat[...], split[...]))
     weights = (wide, narrow, out)
@@ -273,8 +281,12 @@
         end[r] = row
 
 
-def gap_kernel(end, after, split_next, join_next, gap, back, target, fields):
-    store_split(target, 0, permuted(after[...], split_next[...]))
+def gap_kernel(code, end, after, split_next, join_next, gap, back, nat, target, fields):
+    below, above = by_strip(code, after[0:8, :], after[16:24, :])
+    nat[0:8, :] = below
+    nat[8:16, :] = after[8:16, :]
+    nat[16:24, :] = above
+    store_split(target, 0, permuted(nat[...], split_next[...]))
     for r in range(24):
         gap[r] = end[r] - target[r]
     for r in range(8):
@@ -283,35 +295,41 @@
 
 
 def adjoint_kernel(
-    gap, a1, a2, a3, b1, b2, b3, wide, narrow, out, join, adjoint, mismatch, x0, g1, g2, g3, fields
+    gap, a1, a2, a3, b1, b2, b3, wide, narrow, out, join, adjoint, mismatch, x0, g1, g2, g3, fields, gap_rows, sem
 ):
     weights = (wide, narrow, out)
     rows = [gap[r] for r in range(24)]
     for r in range(8):
         fields[r] = rows[8 + r]
+    gap_rows[...] = permuted(joined(fields, 8), join[...])
+    copy = pltpu.make_async_copy(gap_rows, mismatch, sem)
+    copy.start()
     rows = retreat(rows, x0, (b1, b2, b3), (g1, g2, g3), weights, 2)
     rows = retreat(rows, x0, (a1, a2, a3), (g1, g2, g3), weights, 10)
     for r in range(8):
         fields[8 + r] = rows[r]
-    both = permuted(joined(fields, 16), join[...])
-    mismatch[...] = both[0:8]
-    adjoint[...] = both[8:16]
+    adjoint[...] = permuted(joined(fields.at[8:16], 8), join[...])
+    copy.wait()
 
 
 def per_device(initial_states, w_lift, w_second, w_third, w_project, shift_cells, wavenumber):
     segs, strips = lax.axis_size("seg"), lax.axis_size("space")
-    total_rows = ROWS * strips
     own = initial_states[0]
 
-    def fetch(x, by_seg, by_strip):
+    def moved(x, source):
         pairs = []
         for s in range(segs):
             for p in range(strips):
-                pairs.append((((s + by_seg) % segs) * strips + (p + by_strip) % strips, s * strips + p))
+                from_seg, from_strip = source(s, p)
+                pairs.append((from_seg % segs * strips + from_strip % strips, s * strips + p))
         return lax.ppermute(x, ("seg", "space"), pairs)
 
-    m2, m1, p1, p2 = (fetch(own, 0, by) for by in (-2, -1, 1, 2))
-    after = fetch(jnp.concatenate([m1, own, p1], axis=0), 1, 0)
+    m2 = moved(own, lambda s, p: (s, p - 2))
+    across = moved(own, lambda s, p: (s, p - 1 if p % 2 == 0 else p + 1))
+    p2 = moved(own, lambda s, p: (s, p + 2))
+    within = moved(own, lambda s, p: (s, p + 1 if p % 2 == 0 else p - 1))
+    within, m2, across, p2 = lax.optimization_barrier((within, m2, across, p2))
+    after = moved(jnp.concatenate([within, own, across], axis=0), lambda s, p: (s + 1, p))
 
     vmem = pl.BlockSpec(memory_space=pltpu.VMEM)
     smem = pl.BlockSpec(memory_space=pltpu.SMEM)
@@ -330,7 +348,7 @@
 
     nat = jax.ShapeDtypeStruct((ROWS, COLS), f32)
     x0 = pltpu.VMEM((320, LANES), bf16)
-    place = lax.axis_index("space") * ROWS + total_rows - 12
+    code = (lax.axis_index("seg") * strips + lax.axis_index("space")).astype(jnp.int32)[None]
     hbm = pl.BlockSpec(memory_space=pl.ANY)
     perm = pltpu.VMEM((COLS, COLS), bf16)
     wide, narrow, out, force, split, join, split_next, join_next = pl.pallas_call(
@@ -348,35 +366,37 @@
         ],
         cost_estimate=cost(2),
         compiler_params=params(56),
-    )(place.astype(jnp.int32)[None], wavenumber, shift_cells, w_lift.reshape(3, 3, 32), w_second, w_third, w_project.reshape(3, 3, 32))
+    )(code, wavenumber, shift_cells, w_lift.reshape(3, 3, 32), w_second, w_third, w_project.reshape(3, 3, 32))
 
     end, *history = pl.pallas_call(
         forward_kernel,
         out_shape=[fld(24), hid(38), hid(36), hid(34), hid(30), hid(28), hid(26)],
-        in_specs=[vmem] * 10,
+        in_specs=[smem] + [vmem] * 10,
         out_specs=[vmem] * 7,
         scratch_shapes=[pltpu.VMEM((40, COLS), f32), fld(40), x0],
         cost_estimate=cost(6),
         compiler_params=params(8),
-    )(m2, m1, own, p1, p2, wide, narrow, out, force, split)
+    )(code, m2, within, own, across, p2, wide, narrow, out, force, split)
 
     gap, back = pl.pallas_call(
         gap_kernel,
         out_shape=[fld(24), pltpu.VMEM((ROWS, COLS), f32)],
-        in_specs=[vmem] * 4,
+        in_specs=[smem] + [vmem] * 4,
         out_specs=[vmem] * 2,
-        scratch_shapes=[fld(24), fld(8)],
+        scratch_shapes=[pltpu.VMEM((24, COLS), f32), fld(24), fld(8)],
         cost_estimate=cost(1),
         compiler_params=params(8),
-    )(end, after, split_next, join_next)
-    preceding = fetch(back, -1, 0)
+    )(code, end, after, split_next, join_next)
+    preceding = moved(back, lambda s, p: (s - 1, p))
 
     adjoint, mismatch = pl.pallas_call(
         adjoint_kernel,
         out_shape=[pltpu.VMEM((ROWS, COLS), f32), nat],
         in_specs=[vmem] * 11,
-        out_specs=[vmem] * 2,
-        scratch_shapes=[x0, hid(22), hid(22), hid(22), fld(16)],
+        out_specs=[vmem, pl.BlockSpec(memory_space=pl.ANY)],
+        scratch_shapes=[
+            x0, hid(22), hid(22), hid(22), fld(16), pltpu.VMEM((ROWS, COLS), f32), pltpu.SemaphoreType.DMA,
+        ],
         cost_estimate=cost(4),
         compiler_params=params(12),
     )(gap, *history, wide, narrow, out, join)

time: 31.6 us -> 29.8 us (0.943)
  starting transfers between devices: 14.3 us -> 12.5 us
    ppermute x6, starting transfers between devices: 14.3 us -> 12.5 us  [moved(): return lax.ppermute(x, ('seg', 'space'), pairs)]
  transfers between devices with their start and end apart: 6 -> 6, of which waited for: 1 -> 1; matrix products, arithmetic and copies ran while one was open for 0% -> 0% of each run, Pallas kernels for 37% -> 39%
where the time goes in v2:
time: 29.8 us; the launch traced here: 29.7 us
  starting transfers between devices  12.5 us (42%)
  Pallas kernels  11.9 us (40%)
  waiting for transfers between devices  3.31 us (11%)
  between operations  1.39 us (5%)
  other arithmetic  0.62 us (2%)
    ppermute x6, starting transfers between devices, moved(): return lax.ppermute(x, ('seg', 'space'), pairs)  12.5 us
    pallas_call x1, Pallas kernels, per_device(): pl.pallas_call(forward_kernel, out_shape=[fld(24), hid(38), hid(36), hid(...  5.05 us
    pallas_call x1, Pallas kernels, per_device(): pl.pallas_call(adjoint_kernel, out_shape=[pltpu.VMEM((ROWS, COLS), f32),...  4.03 us
    ppermute x6, waiting for transfers between devices, moved(): return lax.ppermute(x, ('seg', 'space'), pairs)  3.31 us
    pallas_call x1, Pallas kernels, per_device(): pl.pallas_call(weights_kernel, out_shape=[pltpu.VMEM((4, 256, 768), bf16)...  2.44 us
    broadcast_in_dim x1, other arithmetic, per_device(): return (updated[None], mismatch[None])  0.61 us
  transfers between devices with their start and end apart: 6, of which 1 were waited for; matrix products, arithmetic and copies ran while one was open for 0% of the time, Pallas kernels for 39%

profile of v2, /device:TPU:0, one launch (start us, length us, event | category | flops | bytes accessed | tf_op | source)
XLA Modules:
  0.0 29.7 jit_solution(9232098865571410413)
XLA Ops:
  0.6 0.1 collective-permute-start
  0.7 0.1 collective-permute-start.1
  0.8 5.1 %collective-permute-start.2 = (f32[8,512]{1,0:T(8,128)}, f32[8,512]{1,0:T(8,128)S(1)}, u32[]{:S(2)}, u32[]{:S(2)}) collective-permute-start(f32[8,512]{1,0:T(8,128)} %bitcast.10), channel_id=1, source_target_pairs={{31,0},{2,1},{1,2},{4,3},{3,4},{6,5},{5,6},{8,7},{7,8},{10,9},{9,1... | collective-permute-start | bytes 49160 | tf_op jit(solution)/shard_map/ppermute | solution.py:325
  6.0 1.8 %collective-permute-start.3 = (f32[8,512]{1,0:T(8,128)}, f32[8,512]{1,0:T(8,128)S(1)}, u32[]{:S(2)}, u32[]{:S(2)}) collective-permute-start(f32[8,512]{1,0:T(8,128)} %bitcast.11), channel_id=1, source_target_pairs={{2,0},{3,1},{4,2},{5,3},{6,4},{7,5},{8,6},{9,7},{10,8},{11,9},{12,... | collective-permute-start | bytes 49160 | tf_op jit(solution)/shard_map/ppermute | solution.py:325
  8.4 0.0 copy-start
  8.4 2.4 %shard_map.86 = (bf16[4,256,768]{2,1,0:T(8,128)(2,1)S(1)}, bf16[2,256,128]{2,1,0:T(8,128)(2,1)S(1)}, bf16[2,32,256]{2,1,0:T(8,128)(2,1)S(1)}, f32[32,128]{1,0:T(...) custom-call(s32[1]{0:T(128)} %bitcast.1.code, ...), custom_call_target="tpu_custom_call" | custom-call | flops 2000000000 | bytes 1000 | tf_op jit(solution)/shard_map/pallas_call | solution.py:354
  10.8 0.0 collective-permute-done.within
  10.8 0.0 collective-permute-done.1.m2
  10.9 0.0 collective-permute-done.2.across
  10.9 0.0 collective-permute-done.3.p2
  10.9 0.0 copy-done
  10.9 5.2 %collective-permute-start.4 = (f32[24,512]{1,0:T(8,128)S(1)}, f32[24,512]{1,0:T(8,128)S(1)}, u32[]{:S(2)}, u32[]{:S(2)}) collective-permute-start(f32[24,512]{1,0:T(8,128)S(1)} %pad_maximum_fusion), channel_id=1, source_target_pairs={{32,0},{33,1},{34,2},{35,3},{36,4},{37,5},{38,6},{39,7},{40,8},{41... | collective-permute-start | bytes 147464 | tf_op jit(solution)/shard_map/ppermute | solution.py:325
  16.1 5.0 %shard_map.87 = (f32[24,8,128]{2,1,0:T(8,128)S(1)}, bf16[38,192,128]{2,1,0:T(8,128)(2,1)S(1)}, bf16[36,192,128]{2,1,0:T(8,128)(2,1)S(1)}, bf16[34,192,128]{2,1,0...) custom-call(s32[1]{0:T(128)} %bitcast.1.code, ...), custom_call_target="tpu_custom_call" | custom-call | flops 6000000000 | bytes 1000 | tf_op jit(solution)/shard_map/pallas_call | solution.py:371
  21.1 0.0 collective-permute-done.4.after
  21.1 0.4 %shard_map.88 = (f32[24,8,128]{2,1,0:T(8,128)S(1)}, f32[8,512]{1,0:T(8,128)S(1)}) custom-call(s32[1]{0:T(128)} %bitcast.1.code, f32[24,8,128]{2,1,0:T(8,128)S(1)} %get-tuple-element.34.end, f32[24,512]{1,0:T(8,128)S(1)} %collective-permute-done.4.after, bf16[512,512]{1,0:T(8,128)(2,1)S(1)} %get-tuple-element.35.split_next, ...), custom_call_target="tpu_custom_call" | custom-call | flops 1000000000 | bytes 1000 | tf_op jit(solution)/shard_map/pallas_call | solution.py:381
  21.5 0.2 collective-permute-start.5
  21.8 4.0 %shard_map.89 = (f32[8,512]{1,0:T(8,128)S(1)}, f32[8,512]{1,0:T(8,128)}) custom-call(f32[24,8,128]{2,1,0:T(8,128)S(1)} %get-tuple-element.37.gap, bf16[38,192,128]{2,1,0:T(8,128)(2,1)S(1)} %get-tuple-element.38.a1, bf16[36,192,128]{2,1,0:T(8,128)(2,1)S(1)} %get-tuple-element.39.a2, bf16[34,192,128]{2,1,0:T(8,128)(2,1)S(1)} %get-tuple-element.40.a3, ...), custom_call_target="tpu_custom_call" | custom-call | flops 4000000000 | bytes 1000 | tf_op jit(solution)/shard_map/pallas_call | solution.py:392
  25.8 3.3 %collective-permute-done.5 = f32[8,512]{1,0:T(8,128)S(1)} collective-permute-done((f32[8,512]{1,0:T(8,128)S(1)}, f32[8,512]{1,0:T(8,128)S(1)}, u32[]{:S(2)}, u32[]{:S(2)}) %collective-permute-start.5) | collective-permute-done | bytes 16416 | tf_op jit(solution)/shard_map/ppermute | solution.py:325
  29.1 0.6 %subtract_bitcast_fusion = f32[1,8,512]{2,1,0:T(8,128)} fusion(f32[8,512]{1,0:T(8,128)S(1)} %get-tuple-element.45, f32[8,512]{1,0:T(8,128)S(1)} %collective-permute-done.5, f32[1,8,512]{2,1,0:T(8,128)S(1)} %copy-done), kind=kLoop, calls=%fused_computation.1 | loop fusion | flops 12288 | bytes 65536 | tf_op jit(solution)/shard_map/broadcast_in_dim | solution.py:404
  (1 shorter events, 0.0 us)
Async XLA Ops:
  0.6 10.2 %collective-permute-start = (f32[8,512]{1,0:T(8,128)}, f32[8,512]{1,0:T(8,128)S(1)}, u32[]{:S(2)}, u32[]{:S(2)}) collective-permute-start(f32[8,512]{1,0:T(8,128)} %bitcast.8), channel_id=1, source_target_pairs={{1,0},{0,1},{3,2},{2,3},{5,4},{4,5},{7,6},{6,7},{9,8},{8,9},{11,10... | collective-permute-start | bytes 49160 | tf_op jit(solution)/shard_map/ppermute | solution.py:325
  0.7 10.1 %collective-permute-start.1 = (f32[8,512]{1,0:T(8,128)}, f32[8,512]{1,0:T(8,128)S(1)}, u32[]{:S(2)}, u32[]{:S(2)}) collective-permute-start(f32[8,512]{1,0:T(8,128)} %bitcast.9), channel_id=1, source_target_pairs={{30,0},{31,1},{0,2},{1,3},{2,4},{3,5},{4,6},{5,7},{6,8},{7,9},{8,1... | collective-permute-start | bytes 49160 | tf_op jit(solution)/shard_map/ppermute | solution.py:325
  0.8 10.0 %collective-permute-start.2 = (f32[8,512]{1,0:T(8,128)}, f32[8,512]{1,0:T(8,128)S(1)}, u32[]{:S(2)}, u32[]{:S(2)}) collective-permute-start(f32[8,512]{1,0:T(8,128)} %bitcast.10), channel_id=1, source_target_pairs={{31,0},{2,1},{1,2},{4,3},{3,4},{6,5},{5,6},{8,7},{7,8},{10,9},{9,1... | collective-permute-start | bytes 49160 | tf_op jit(solution)/shard_map/ppermute | solution.py:325
  6.0 4.9 %collective-permute-start.3 = (f32[8,512]{1,0:T(8,128)}, f32[8,512]{1,0:T(8,128)S(1)}, u32[]{:S(2)}, u32[]{:S(2)}) collective-permute-start(f32[8,512]{1,0:T(8,128)} %bitcast.11), channel_id=1, source_target_pairs={{2,0},{3,1},{4,2},{5,3},{6,4},{7,5},{8,6},{9,7},{10,8},{11,9},{12,... | collective-permute-start | bytes 49160 | tf_op jit(solution)/shard_map/ppermute | solution.py:325
  8.4 2.5 %copy-start = (f32[1,8,512]{2,1,0:T(8,128)S(1)}, f32[1,8,512]{2,1,0:T(8,128)}, u32[]{:S(2)}) copy-start(f32[1,8,512]{2,1,0:T(8,128)} %param.7) | copy-start | bytes 49156
  10.9 10.2 %collective-permute-start.4 = (f32[24,512]{1,0:T(8,128)S(1)}, f32[24,512]{1,0:T(8,128)S(1)}, u32[]{:S(2)}, u32[]{:S(2)}) collective-permute-start(f32[24,512]{1,0:T(8,128)S(1)} %pad_maximum_fusion), channel_id=1, source_target_pairs={{32,0},{33,1},{34,2},{35,3},{36,4},{37,5},{38,6},{39,7},{40,8},{41... | collective-permute-start | bytes 147464 | tf_op jit(solution)/shard_map/ppermute | solution.py:325
  21.5 7.6 %collective-permute-start.5 = (f32[8,512]{1,0:T(8,128)S(1)}, f32[8,512]{1,0:T(8,128)S(1)}, u32[]{:S(2)}, u32[]{:S(2)}) collective-permute-start(f32[8,512]{1,0:T(8,128)S(1)} %get-tuple-element.46), channel_id=1, source_target_pairs={{224,0},{225,1},{226,2},{227,3},{228,4},{229,5},{230,6},{231,7},{2... | collective-permute-start | bytes 49160 | tf_op jit(solution)/shard_map/ppermute | solution.py:325

commit v3 on v2

--- a/solution.py
+++ b/solution.py
@@ -179,9 +179,26 @@
     return rows, [turned[:, t : t + 1] for t in range(9)]
 
 
+def lift_weight(cols, flip, dst):
+    lane = lax.broadcasted_iota(jnp.int32, (32, LANES), 1)
+    taps = [jnp.broadcast_to(col, (32, LANES)) for col in cols]
+    for p in range(8):
+        index = jnp.where(lane < 32, tap_index((lane >> 3) - p // 4, (lane & 7) - p % 4), -1)
+        dst[32 * p : 32 * p + 32, :] = chosen(taps, index, flip).astype(bf16)
+
+
+def out_weight(rows, flip):
+    row = lax.broadcasted_iota(jnp.int32, (32, 256), 0)
+    lane = lax.broadcasted_iota(jnp.int32, (32, 256), 1)
+    index = jnp.where((row & 7) < 6, tap_index((lane >> 7) - (row >> 3) + 2, ((lane >> 5) & 3) - (row & 7) + 2), -1)
+    taps = [jnp.broadcast_to(jnp.concatenate([r] * 8, axis=1), (32, 256)) for r in rows]
+    return chosen(taps, index, flip).astype(bf16)
+
+
 def weights_kernel(
-    code, number_hbm, shift_hbm, lift_hbm, second_hbm, third_hbm, project_hbm, wide, narrow, out, force, split, join,
-    split_next, join_next, number, shift, lift_ref, second, third, project_ref, sems,
+    number_hbm, shift_hbm, lift_hbm, second_hbm, third_hbm, project_hbm,
+    wide, narrow, out, force, split, split_next, join_next, lift_ref, second, third, project_ref,
+    number, shift, sems,
 ):
     pairs = (
         (number_hbm, number), (shift_hbm, shift), (lift_hbm, lift_ref), (project_hbm, project_ref),
@@ -191,35 +208,20 @@
     for copy in copies:
         copy.start()
     split[...] = split_perm(0)
-    join[...] = join_perm(0)
-    for copy in copies:
+    for copy in copies[2:]:
+        copy.wait()
+    for layer, taps in ((0, second), (1, third)):
+        hidden_weight(placed([taps[t // 3, t % 3].astype(f32).T for t in range(9)]), wide, layer)
+    lift_weight(rows_and_columns(lift_ref)[1], False, narrow)
+    out[...] = out_weight(rows_and_columns(project_ref)[0], False)
+    for copy in copies[:2]:
         copy.wait()
     split_next[...] = split_perm(shift[0])
     join_next[...] = join_perm(shift[0])
-    row = ROWS * (code[0] & 31) + NY - 12 + lax.broadcasted_iota(jnp.int32, (32, LANES), 0)
+    row = ROWS * lax.axis_index("space") + NY - 12 + lax.broadcasted_iota(jnp.int32, (32, LANES), 0)
     first = ((number[0] * row) & (NY - 1)).astype(f32)
     other = ((number[1] * row) & (NY - 1)).astype(f32)
     force[...] = jnp.cos(2.0 * math.pi * first / NY) + 0.5 * jnp.sin(2.0 * math.pi * other / NY)
-    for layer, taps in ((0, second), (1, third)):
-        hidden_weight(placed([taps[t // 3, t % 3].astype(f32).T for t in range(9)]), wide, layer)
-    for layer, taps in ((2, third), (3, second)):
-        hidden_weight(placed([taps[2 - t // 3, 2 - t % 3].astype(f32) for t in range(9)]), wide, layer)
-
-    lift_rows, lift_cols = rows_and_columns(lift_ref)
-    project_rows, project_cols = rows_and_columns(project_ref)
-    for layer, cols, flip in ((0, lift_cols, False), (1, project_cols, True)):
-        lane = lax.broadcasted_iota(jnp.int32, (32, LANES), 1)
-        taps = [jnp.broadcast_to(col, (32, LANES)) for col in cols]
-        for p in range(8):
-            index = jnp.where(lane < 32, tap_index((lane >> 3) - p // 4, (lane & 7) - p % 4), -1)
-            narrow[layer, 32 * p : 32 * p + 32, :] = chosen(taps, index, flip).astype(bf16)
-
-    row = lax.broadcasted_iota(jnp.int32, (32, 256), 0)
-    lane = lax.broadcasted_iota(jnp.int32, (32, 256), 1)
-    index = jnp.where((row & 7) < 6, tap_index((lane >> 7) - (row >> 3) + 2, ((lane >> 5) & 3) - (row & 7) + 2), -1)
-    for layer, rows, flip in ((0, project_rows, False), (1, lift_rows, True)):
-        taps = [jnp.broadcast_to(jnp.concatenate([r] * 8, axis=1), (32, 256)) for r in rows]
-        out[layer] = chosen(taps, index, flip).astype(bf16)
 
 
 def tanh_of(y, row):
@@ -230,10 +232,10 @@
     count = len(rows)
     wide, narrow, out = weights
     set_lift(x0, rows)
-    lift(x0, h1, narrow[0, :, 0:32], count - 2, tanh_of)
+    lift(x0, h1, narrow[:, 0:32], count - 2, tanh_of)
     hidden(h1, h2, wide.at[0], count - 4, tanh_of)
     hidden(h2, h3, wide.at[1], count - 6, tanh_of)
-    pushed = project(h3, out[0], count - 6)
+    pushed = project(h3, out[...], count - 6)
     return [
         w + time_step * (t + force[first + r : first + r + 1, :] - drag_rate * w)
         for r, (w, t) in enumerate(zip(rows[4:-4], pushed))
@@ -248,27 +250,29 @@
     return finish
 
 
-def retreat(rows, x0, history, made, weights, offset):
+def retreat(rows, x0, history, made, weights, offset, between=None):
     count = len(rows)
     wide, narrow, out = weights
     (h1, h2, h3), (g1, g2, g3) = history, made
     set_lift(x0, [time_step * l for l in rows])
-    lift(x0, g3, narrow[1, :, 0:32], count - 2, masked_by(h3, offset))
-    hidden(g3, g2, wide.at[2], count - 4, masked_by(h2, offset + 2))
-    hidden(g2, g1, wide.at[3], count - 6, masked_by(h1, offset + 4))
-    pulled = project(g1, out[1], count - 6)
+    lift(x0, g3, narrow[:, 0:32], count - 2, masked_by(h3, offset))
+    if between is not None:
+        between()
+    hidden(g3, g2, wide.at[0], count - 4, masked_by(h2, offset + 2))
+    hidden(g2, g1, wide.at[1], count - 6, masked_by(h1, offset + 4))
+    pulled = project(g1, out[...], count - 6)
     return [l * (1.0 - time_step * drag_rate) + t for l, t in zip(rows[4:-4], pulled)]
 
 
-def by_strip(code, within, across):
-    even = (code[0] & 1) == 0
+def by_strip(within, across):
+    even = lax.rem(lax.axis_index("space"), 2) == 0
     return jnp.where(even, across, within), jnp.where(even, within, across)
 
 
 def forward_kernel(
-    code, m2, within, own, across, p2, wide, narrow, out, force, split, end, a1, a2, a3, b1, b2, b3, nat, field, x0
+    m2, within, own, across, p2, wide, narrow, out, force, split, end, a1, a2, a3, b1, b2, b3, nat, field, x0
 ):
-    m1, p1 = by_strip(code, within[...], across[...])
+    m1, p1 = by_strip(within[...], across[...])
     nat[0:8, :] = m2[...]
     nat[8:16, :] = m1
     nat[16:24, :] = own[...]
@@ -281,8 +285,8 @@
         end[r] = row
 
 
-def gap_kernel(code, end, after, split_next, join_next, gap, back, nat, target, fields):
-    below, above = by_strip(code, after[0:8, :], after[16:24, :])
+def gap_kernel(end, after, split_next, join_next, gap, back, nat, target, fields):
+    below, above = by_strip(after[0:8, :], after[16:24, :])
     nat[0:8, :] = below
     nat[8:16, :] = after[8:16, :]
     nat[16:24, :] = above
@@ -295,16 +299,25 @@
 
 
 def adjoint_kernel(
-    gap, a1, a2, a3, b1, b2, b3, wide, narrow, out, join, adjoint, mismatch, x0, g1, g2, g3, fields, gap_rows, sem
+    gap, a1, a2, a3, b1, b2, b3, lift_ref, second, third, project_ref, adjoint, mismatch,
+    wide, narrow, out, join, x0, g1, g2, g3, fields, gap_rows, sem,
 ):
     weights = (wide, narrow, out)
+    lift_weight(rows_and_columns(project_ref)[1], True, narrow)
     rows = [gap[r] for r in range(24)]
+    join[...] = join_perm(0)
     for r in range(8):
         fields[r] = rows[8 + r]
     gap_rows[...] = permuted(joined(fields, 8), join[...])
     copy = pltpu.make_async_copy(gap_rows, mismatch, sem)
     copy.start()
-    rows = retreat(rows, x0, (b1, b2, b3), (g1, g2, g3), weights, 2)
+
+    def build():
+        for layer, taps in ((0, third), (1, second)):
+            hidden_weight(placed([taps[2 - t // 3, 2 - t % 3].astype(f32) for t in range(9)]), wide, layer)
+        out[...] = out_weight(rows_and_columns(lift_ref)[0], True)
+
+    rows = retreat(rows, x0, (b1, b2, b3), (g1, g2, g3), weights, 2, build)
     rows = retreat(rows, x0, (a1, a2, a3), (g1, g2, g3), weights, 10)
     for r in range(8):
         fields[8 + r] = rows[r]
@@ -332,7 +345,6 @@
     after = moved(jnp.concatenate([within, own, across], axis=0), lambda s, p: (s + 1, p))
 
     vmem = pl.BlockSpec(memory_space=pltpu.VMEM)
-    smem = pl.BlockSpec(memory_space=pltpu.SMEM)
 
     def hid(rows):
         return pltpu.VMEM((rows, 192, LANES), bf16)
@@ -348,45 +360,44 @@
 
     nat = jax.ShapeDtypeStruct((ROWS, COLS), f32)
     x0 = pltpu.VMEM((320, LANES), bf16)
-    code = (lax.axis_index("seg") * strips + lax.axis_index("space")).astype(jnp.int32)[None]
     hbm = pl.BlockSpec(memory_space=pl.ANY)
     perm = pltpu.VMEM((COLS, COLS), bf16)
-    wide, narrow, out, force, split, join, split_next, join_next = pl.pallas_call(
+    taps, hidden_taps = (3, 3, 32), (3, 3, 32, 32)
+    wide_shape, narrow_shape, out_shape = (
+        pltpu.VMEM((2, 256, 768), bf16), pltpu.VMEM((256, LANES), bf16), pltpu.VMEM((32, 256), bf16)
+    )
+    wide, narrow, out, force, split, split_next, join_next, *raw = pl.pallas_call(
         weights_kernel,
         out_shape=[
-            pltpu.VMEM((4, 256, 768), bf16), pltpu.VMEM((2, 256, LANES), bf16), pltpu.VMEM((2, 32, 256), bf16),
-            pltpu.VMEM((32, LANES), f32), perm, perm, perm, perm,
+            wide_shape, narrow_shape, out_shape, pltpu.VMEM((32, LANES), f32), perm, perm, perm,
+            pltpu.VMEM(taps, bf16), pltpu.VMEM(hidden_taps, bf16), pltpu.VMEM(hidden_taps, bf16), pltpu.VMEM(taps, bf16),
         ],
-        in_specs=[smem] + [hbm] * 6,
-        out_specs=[vmem] * 8,
-        scratch_shapes=[
-            pltpu.SMEM((2,), jnp.int32), pltpu.SMEM((1,), jnp.int32), pltpu.VMEM((3, 3, 32), bf16),
-            pltpu.VMEM((3, 3, 32, 32), bf16), pltpu.VMEM((3, 3, 32, 32), bf16), pltpu.VMEM((3, 3, 32), bf16),
-            pltpu.SemaphoreType.DMA((6,)),
-        ],
+        in_specs=[hbm] * 6,
+        out_specs=[vmem] * 11,
+        scratch_shapes=[pltpu.SMEM((2,), jnp.int32), pltpu.SMEM((1,), jnp.int32), pltpu.SemaphoreType.DMA((6,))],
         cost_estimate=cost(2),
         compiler_params=params(56),
-    )(code, wavenumber, shift_cells, w_lift.reshape(3, 3, 32), w_second, w_third, w_project.reshape(3, 3, 32))
+    )(wavenumber, shift_cells, w_lift.reshape(taps), w_second, w_third, w_project.reshape(taps))
 
     end, *history = pl.pallas_call(
         forward_kernel,
         out_shape=[fld(24), hid(38), hid(36), hid(34), hid(30), hid(28), hid(26)],
-        in_specs=[smem] + [vmem] * 10,
+        in_specs=[vmem] * 10,
         out_specs=[vmem] * 7,
         scratch_shapes=[pltpu.VMEM((40, COLS), f32), fld(40), x0],
         cost_estimate=cost(6),
         compiler_params=params(8),
-    )(code, m2, within, own, across, p2, wide, narrow, out, force, split)
+    )(m2, within, own, across, p2, wide, narrow, out, force, split)
 
     gap, back = pl.pallas_call(
         gap_kernel,
         out_shape=[fld(24), pltpu.VMEM((ROWS, COLS), f32)],
-        in_specs=[smem] + [vmem] * 4,
+        in_specs=[vmem] * 4,
         out_specs=[vmem] * 2,
         scratch_shapes=[pltpu.VMEM((24, COLS), f32), fld(24), fld(8)],
         cost_estimate=cost(1),
         compiler_params=params(8),
-    )(code, end, after, split_next, join_next)
+    )(end, after, split_next, join_next)
     preceding = moved(back, lambda s, p: (s - 1, p))
 
     adjoint, mismatch = pl.pallas_call(
@@ -395,11 +406,12 @@
         in_specs=[vmem] * 11,
         out_specs=[vmem, pl.BlockSpec(memory_space=pl.ANY)],
         scratch_shapes=[
+            wide_shape, narrow_shape, out_shape, perm,
             x0, hid(22), hid(22), hid(22), fld(16), pltpu.VMEM((ROWS, COLS), f32), pltpu.SemaphoreType.DMA,
         ],
         cost_estimate=cost(4),
         compiler_params=params(12),
-    )(gap, *history, wide, narrow, out, join)
+    )(gap, *history, *raw)
     updated = own - learn_rate * (adjoint - preceding)
     return updated[None], mismatch[None]
 

time: 29.8 us -> 29.6 us (level)
  waiting for transfers between devices: 3.31 us -> 2.93 us
    pallas_call x1, Pallas kernels: 2.44 us -> 2.04 us  [per_device(): pl.pallas_call(weights_kernel, out_shape=[wide_shape, narrow_shape, out_s...]
    ppermute x6, waiting for transfers between devices: 3.31 us -> 2.93 us  [moved(): return lax.ppermute(x, ('seg', 'space'), pairs)]
    pallas_call x1, Pallas kernels: 4.03 us -> 4.41 us  [per_device(): pl.pallas_call(adjoint_kernel, out_shape=[pltpu.VMEM((ROWS, COLS), f32),...]
  transfers between devices with their start and end apart: 6 -> 6, of which waited for: 1 -> 1; matrix products, arithmetic and copies ran while one was open for 0% -> 0% of each run, Pallas kernels for 39% -> 40%
where the time goes in v3:
time: 29.6 us; the launch traced here: 29.4 us
  starting transfers between devices  12.5 us (42%)
  Pallas kernels  12 us (41%)
  waiting for transfers between devices  2.93 us (10%)
  between operations  1.39 us (5%)
  other arithmetic  0.62 us (2%)
    ppermute x6, starting transfers between devices, moved(): return lax.ppermute(x, ('seg', 'space'), pairs)  12.5 us
    pallas_call x1, Pallas kernels, per_device(): pl.pallas_call(forward_kernel, out_shape=[fld(24), hid(38), hid(36), hid(...  5.17 us
    pallas_call x1, Pallas kernels, per_device(): pl.pallas_call(adjoint_kernel, out_shape=[pltpu.VMEM((ROWS, COLS), f32),...  4.41 us
    ppermute x6, waiting for transfers between devices, moved(): return lax.ppermute(x, ('seg', 'space'), pairs)  2.93 us
    pallas_call x1, Pallas kernels, per_device(): pl.pallas_call(weights_kernel, out_shape=[wide_shape, narrow_shape, out_s...  2.04 us
    broadcast_in_dim x1, other arithmetic, per_device(): return (updated[None], mismatch[None])  0.61 us
  transfers between devices with their start and end apart: 6, of which 1 were waited for; matrix products, arithmetic and copies ran while one was open for 0% of the time, Pallas kernels for 40%

profile of v3, /device:TPU:0, one launch (start us, length us, event | category | flops | bytes accessed | tf_op | source)
XLA Modules:
  0.0 29.4 jit_solution(18246237607857515874)
XLA Ops:
  0.6 0.1 collective-permute-start
  0.7 0.1 collective-permute-start.1
  0.8 5.1 %collective-permute-start.2 = (f32[8,512]{1,0:T(8,128)}, f32[8,512]{1,0:T(8,128)S(1)}, u32[]{:S(2)}, u32[]{:S(2)}) collective-permute-start(f32[8,512]{1,0:T(8,128)} %bitcast.9), channel_id=1, source_target_pairs={{31,0},{2,1},{1,2},{4,3},{3,4},{6,5},{5,6},{8,7},{7,8},{10,9},{9,1... | collective-permute-start | bytes 49160 | tf_op jit(solution)/shard_map/ppermute | solution.py:338
  6.0 1.8 %collective-permute-start.3 = (f32[8,512]{1,0:T(8,128)}, f32[8,512]{1,0:T(8,128)S(1)}, u32[]{:S(2)}, u32[]{:S(2)}) collective-permute-start(f32[8,512]{1,0:T(8,128)} %bitcast.10), channel_id=1, source_target_pairs={{2,0},{3,1},{4,2},{5,3},{6,4},{7,5},{8,6},{9,7},{10,8},{11,9},{12,... | collective-permute-start | bytes 49160 | tf_op jit(solution)/shard_map/ppermute | solution.py:338
  8.4 0.0 copy-start
  8.4 2.0 %shard_map.86 = (bf16[2,256,768]{2,1,0:T(8,128)(2,1)S(1)}, bf16[256,128]{1,0:T(8,128)(2,1)S(1)}, bf16[32,256]{1,0:T(8,128)(2,1)S(1)}, f32[32,128]{1,0:T(8,128)S(...) custom-call(s32[2]{0:T(128)} %number_hbm.1, ...), custom_call_target="tpu_custom_call" | custom-call | flops 2000000000 | bytes 1000 | tf_op jit(solution)/shard_map/pallas_call | solution.py:369
  10.4 0.0 collective-permute-done.within
  10.4 0.0 collective-permute-done.1.m2
  10.5 0.0 collective-permute-done.2.across
  10.5 0.0 collective-permute-done.3.p2
  10.5 0.0 copy-done
  10.5 5.2 %collective-permute-start.4 = (f32[24,512]{1,0:T(8,128)S(1)}, f32[24,512]{1,0:T(8,128)S(1)}, u32[]{:S(2)}, u32[]{:S(2)}) collective-permute-start(f32[24,512]{1,0:T(8,128)S(1)} %pad_maximum_fusion), channel_id=1, source_target_pairs={{32,0},{33,1},{34,2},{35,3},{36,4},{37,5},{38,6},{39,7},{40,8},{41... | collective-permute-start | bytes 147464 | tf_op jit(solution)/shard_map/ppermute | solution.py:338
  15.7 5.2 %shard_map.87 = (f32[24,8,128]{2,1,0:T(8,128)S(1)}, bf16[38,192,128]{2,1,0:T(8,128)(2,1)S(1)}, bf16[36,192,128]{2,1,0:T(8,128)(2,1)S(1)}, bf16[34,192,128]{2,1,0...) custom-call(f32[8,512]{1,0:T(8,128)S(1)} %collective-permute-done.1., ...), custom_call_target="tpu_custom_call" | custom-call | flops 6000000000 | bytes 1000 | tf_op jit(solution)/shard_map/pallas_call | solution.py:382
  20.9 0.0 collective-permute-done.4.after
  20.9 0.4 %shard_map.88 = (f32[24,8,128]{2,1,0:T(8,128)S(1)}, f32[8,512]{1,0:T(8,128)S(1)}) custom-call(f32[24,8,128]{2,1,0:T(8,128)S(1)} %get-tuple-element.37.end, f32[24,512]{1,0:T(8,128)S(1)} %collective-permute-done.4.after, bf16[512,512]{1,0:T(8,128)(2,1)S(1)} %get-tuple-element.38.split_next, bf16[512,512]{1,0:T(8,128)(2,1)S(1)} %get-tuple-element.39.join_next), custom_call_target="tpu_custom_call" | custom-call | flops 1000000000 | bytes 1000 | tf_op jit(solution)/shard_map/pallas_call | solution.py:392
  21.2 0.2 collective-permute-start.5
  21.5 4.4 %shard_map.89 = (f32[8,512]{1,0:T(8,128)S(1)}, f32[8,512]{1,0:T(8,128)}) custom-call(f32[24,8,128]{2,1,0:T(8,128)S(1)} %get-tuple-element.40.gap, bf16[38,192,128]{2,1,0:T(8,128)(2,1)S(1)} %get-tuple-element.41.a1, bf16[36,192,128]{2,1,0:T(8,128)(2,1)S(1)} %get-tuple-element.42.a2, bf16[34,192,128]{2,1,0:T(8,128)(2,1)S(1)} %get-tuple-element.43.a3, ...), custom_call_target="tpu_custom_call" | custom-call | flops 4000000000 | bytes 1000 | tf_op jit(solution)/shard_map/pallas_call | solution.py:403
  25.9 2.9 %collective-permute-done.5 = f32[8,512]{1,0:T(8,128)S(1)} collective-permute-done((f32[8,512]{1,0:T(8,128)S(1)}, f32[8,512]{1,0:T(8,128)S(1)}, u32[]{:S(2)}, u32[]{:S(2)}) %collective-permute-start.5) | collective-permute-done | bytes 16416 | tf_op jit(solution)/shard_map/ppermute | solution.py:338
  28.8 0.6 %subtract_bitcast_fusion = f32[1,8,512]{2,1,0:T(8,128)} fusion(f32[8,512]{1,0:T(8,128)S(1)} %get-tuple-element.51, f32[8,512]{1,0:T(8,128)S(1)} %collective-permute-done.5, f32[1,8,512]{2,1,0:T(8,128)S(1)} %copy-done), kind=kLoop, calls=%fused_computation.1 | loop fusion | flops 12288 | bytes 65536 | tf_op jit(solution)/shard_map/broadcast_in_dim | solution.py:416
  (1 shorter events, 0.0 us)
Async XLA Ops:
  0.6 9.8 %collective-permute-start = (f32[8,512]{1,0:T(8,128)}, f32[8,512]{1,0:T(8,128)S(1)}, u32[]{:S(2)}, u32[]{:S(2)}) collective-permute-start(f32[8,512]{1,0:T(8,128)} %bitcast.7), channel_id=1, source_target_pairs={{1,0},{0,1},{3,2},{2,3},{5,4},{4,5},{7,6},{6,7},{9,8},{8,9},{11,10... | collective-permute-start | bytes 49160 | tf_op jit(solution)/shard_map/ppermute | solution.py:338
  0.7 9.7 %collective-permute-start.1 = (f32[8,512]{1,0:T(8,128)}, f32[8,512]{1,0:T(8,128)S(1)}, u32[]{:S(2)}, u32[]{:S(2)}) collective-permute-start(f32[8,512]{1,0:T(8,128)} %bitcast.8), channel_id=1, source_target_pairs={{30,0},{31,1},{0,2},{1,3},{2,4},{3,5},{4,6},{5,7},{6,8},{7,9},{8,1... | collective-permute-start | bytes 49160 | tf_op jit(solution)/shard_map/ppermute | solution.py:338
  0.8 9.6 %collective-permute-start.2 = (f32[8,512]{1,0:T(8,128)}, f32[8,512]{1,0:T(8,128)S(1)}, u32[]{:S(2)}, u32[]{:S(2)}) collective-permute-start(f32[8,512]{1,0:T(8,128)} %bitcast.9), channel_id=1, source_target_pairs={{31,0},{2,1},{1,2},{4,3},{3,4},{6,5},{5,6},{8,7},{7,8},{10,9},{9,1... | collective-permute-start | bytes 49160 | tf_op jit(solution)/shard_map/ppermute | solution.py:338
  6.0 4.5 %collective-permute-start.3 = (f32[8,512]{1,0:T(8,128)}, f32[8,512]{1,0:T(8,128)S(1)}, u32[]{:S(2)}, u32[]{:S(2)}) collective-permute-start(f32[8,512]{1,0:T(8,128)} %bitcast.10), channel_id=1, source_target_pairs={{2,0},{3,1},{4,2},{5,3},{6,4},{7,5},{8,6},{9,7},{10,8},{11,9},{12,... | collective-permute-start | bytes 49160 | tf_op jit(solution)/shard_map/ppermute | solution.py:338
  8.4 2.1 %copy-start = (f32[1,8,512]{2,1,0:T(8,128)S(1)}, f32[1,8,512]{2,1,0:T(8,128)}, u32[]{:S(2)}) copy-start(f32[1,8,512]{2,1,0:T(8,128)} %param.7) | copy-start | bytes 49156
  10.5 10.4 %collective-permute-start.4 = (f32[24,512]{1,0:T(8,128)S(1)}, f32[24,512]{1,0:T(8,128)S(1)}, u32[]{:S(2)}, u32[]{:S(2)}) collective-permute-start(f32[24,512]{1,0:T(8,128)S(1)} %pad_maximum_fusion), channel_id=1, source_target_pairs={{32,0},{33,1},{34,2},{35,3},{36,4},{37,5},{38,6},{39,7},{40,8},{41... | collective-permute-start | bytes 147464 | tf_op jit(solution)/shard_map/ppermute | solution.py:338
  21.2 7.6 %collective-permute-start.5 = (f32[8,512]{1,0:T(8,128)S(1)}, f32[8,512]{1,0:T(8,128)S(1)}, u32[]{:S(2)}, u32[]{:S(2)}) collective-permute-start(f32[8,512]{1,0:T(8,128)S(1)} %get-tuple-element.52), channel_id=1, source_target_pairs={{224,0},{225,1},{226,2},{227,3},{228,4},{229,5},{230,6},{231,7},{2... | collective-permute-start | bytes 49160 | tf_op jit(solution)/shard_map/ppermute | solution.py:338

commit v4 on v3

--- a/solution.py
+++ b/solution.py
@@ -305,17 +305,17 @@
     weights = (wide, narrow, out)
     lift_weight(rows_and_columns(project_ref)[1], True, narrow)
     rows = [gap[r] for r in range(24)]
-    join[...] = join_perm(0)
-    for r in range(8):
-        fields[r] = rows[8 + r]
-    gap_rows[...] = permuted(joined(fields, 8), join[...])
     copy = pltpu.make_async_copy(gap_rows, mismatch, sem)
-    copy.start()
 
     def build():
         for layer, taps in ((0, third), (1, second)):
             hidden_weight(placed([taps[2 - t // 3, 2 - t % 3].astype(f32) for t in range(9)]), wide, layer)
         out[...] = out_weight(rows_and_columns(lift_ref)[0], True)
+        join[...] = join_perm(0)
+        for r in range(8):
+            fields[r] = gap[8 + r]
+        gap_rows[...] = permuted(joined(fields, 8), join[...])
+        copy.start()
 
     rows = retreat(rows, x0, (b1, b2, b3), (g1, g2, g3), weights, 2, build)
     rows = retreat(rows, x0, (a1, a2, a3), (g1, g2, g3), weights, 10)

time: 29.6 us -> 29.6 us (level)
  no operation moved by 1% of the time
where the time goes in v4:
time: 29.6 us; the launch traced here: 29.4 us
  starting transfers between devices  12.5 us (42%)
  Pallas kernels  12.1 us (41%)
  waiting for transfers between devices  2.84 us (10%)
  between operations  1.39 us (5%)
  other arithmetic  0.62 us (2%)
    ppermute x6, starting transfers between devices, moved(): return lax.ppermute(x, ('seg', 'space'), pairs)  12.5 us
    pallas_call x1, Pallas kernels, per_device(): pl.pallas_call(forward_kernel, out_shape=[fld(24), hid(38), hid(36), hid(...  5.17 us
    pallas_call x1, Pallas kernels, per_device(): pl.pallas_call(adjoint_kernel, out_shape=[pltpu.VMEM((ROWS, COLS), f32),...  4.5 us
    ppermute x6, waiting for transfers between devices, moved(): return lax.ppermute(x, ('seg', 'space'), pairs)  2.84 us
    pallas_call x1, Pallas kernels, per_device(): pl.pallas_call(weights_kernel, out_shape=[wide_shape, narrow_shape, out_s...  2.04 us
    broadcast_in_dim x1, other arithmetic, per_device(): return (updated[None], mismatch[None])  0.61 us
  transfers between devices with their start and end apart: 6, of which 1 were waited for; matrix products, arithmetic and copies ran while one was open for 0% of the time, Pallas kernels for 40%

profile of v4, /device:TPU:0, one launch (start us, length us, event | category | flops | bytes accessed | tf_op | source)
XLA Modules:
  0.0 29.4 jit_solution(10871625041643372326)
XLA Ops:
  0.6 0.1 collective-permute-start
  0.7 0.1 collective-permute-start.1
  0.8 5.1 %collective-permute-start.2 = (f32[8,512]{1,0:T(8,128)}, f32[8,512]{1,0:T(8,128)S(1)}, u32[]{:S(2)}, u32[]{:S(2)}) collective-permute-start(f32[8,512]{1,0:T(8,128)} %bitcast.9), channel_id=1, source_target_pairs={{31,0},{2,1},{1,2},{4,3},{3,4},{6,5},{5,6},{8,7},{7,8},{10,9},{9,1... | collective-permute-start | bytes 49160 | tf_op jit(solution)/shard_map/ppermute | solution.py:338
  6.0 1.8 %collective-permute-start.3 = (f32[8,512]{1,0:T(8,128)}, f32[8,512]{1,0:T(8,128)S(1)}, u32[]{:S(2)}, u32[]{:S(2)}) collective-permute-start(f32[8,512]{1,0:T(8,128)} %bitcast.10), channel_id=1, source_target_pairs={{2,0},{3,1},{4,2},{5,3},{6,4},{7,5},{8,6},{9,7},{10,8},{11,9},{12,... | collective-permute-start | bytes 49160 | tf_op jit(solution)/shard_map/ppermute | solution.py:338
  8.4 0.0 copy-start
  8.4 2.0 %shard_map.86 = (bf16[2,256,768]{2,1,0:T(8,128)(2,1)S(1)}, bf16[256,128]{1,0:T(8,128)(2,1)S(1)}, bf16[32,256]{1,0:T(8,128)(2,1)S(1)}, f32[32,128]{1,0:T(8,128)S(...) custom-call(s32[2]{0:T(128)} %number_hbm.1, ...), custom_call_target="tpu_custom_call" | custom-call | flops 2000000000 | bytes 1000 | tf_op jit(solution)/shard_map/pallas_call | solution.py:369
  10.4 0.0 collective-permute-done.within
  10.4 0.0 collective-permute-done.1.m2
  10.5 0.0 collective-permute-done.2.across
  10.5 0.0 collective-permute-done.3.p2
  10.5 0.0 copy-done
  10.5 5.2 %collective-permute-start.4 = (f32[24,512]{1,0:T(8,128)S(1)}, f32[24,512]{1,0:T(8,128)S(1)}, u32[]{:S(2)}, u32[]{:S(2)}) collective-permute-start(f32[24,512]{1,0:T(8,128)S(1)} %pad_maximum_fusion), channel_id=1, source_target_pairs={{32,0},{33,1},{34,2},{35,3},{36,4},{37,5},{38,6},{39,7},{40,8},{41... | collective-permute-start | bytes 147464 | tf_op jit(solution)/shard_map/ppermute | solution.py:338
  15.7 5.2 %shard_map.87 = (f32[24,8,128]{2,1,0:T(8,128)S(1)}, bf16[38,192,128]{2,1,0:T(8,128)(2,1)S(1)}, bf16[36,192,128]{2,1,0:T(8,128)(2,1)S(1)}, bf16[34,192,128]{2,1,0...) custom-call(f32[8,512]{1,0:T(8,128)S(1)} %collective-permute-done.1., ...), custom_call_target="tpu_custom_call" | custom-call | flops 6000000000 | bytes 1000 | tf_op jit(solution)/shard_map/pallas_call | solution.py:382
  20.9 0.0 collective-permute-done.4.after
  20.9 0.4 %shard_map.88 = (f32[24,8,128]{2,1,0:T(8,128)S(1)}, f32[8,512]{1,0:T(8,128)S(1)}) custom-call(f32[24,8,128]{2,1,0:T(8,128)S(1)} %get-tuple-element.37.end, f32[24,512]{1,0:T(8,128)S(1)} %collective-permute-done.4.after, bf16[512,512]{1,0:T(8,128)(2,1)S(1)} %get-tuple-element.38.split_next, bf16[512,512]{1,0:T(8,128)(2,1)S(1)} %get-tuple-element.39.join_next), custom_call_target="tpu_custom_call" | custom-call | flops 1000000000 | bytes 1000 | tf_op jit(solution)/shard_map/pallas_call | solution.py:392
  21.2 0.2 collective-permute-start.5
  21.5 4.5 %shard_map.89 = (f32[8,512]{1,0:T(8,128)S(1)}, f32[8,512]{1,0:T(8,128)}) custom-call(f32[24,8,128]{2,1,0:T(8,128)S(1)} %get-tuple-element.40.gap, bf16[38,192,128]{2,1,0:T(8,128)(2,1)S(1)} %get-tuple-element.41.a1, bf16[36,192,128]{2,1,0:T(8,128)(2,1)S(1)} %get-tuple-element.42.a2, bf16[34,192,128]{2,1,0:T(8,128)(2,1)S(1)} %get-tuple-element.43.a3, ...), custom_call_target="tpu_custom_call" | custom-call | flops 4000000000 | bytes 1000 | tf_op jit(solution)/shard_map/pallas_call | solution.py:403
  26.0 2.8 %collective-permute-done.5 = f32[8,512]{1,0:T(8,128)S(1)} collective-permute-done((f32[8,512]{1,0:T(8,128)S(1)}, f32[8,512]{1,0:T(8,128)S(1)}, u32[]{:S(2)}, u32[]{:S(2)}) %collective-permute-start.5) | collective-permute-done | bytes 16416 | tf_op jit(solution)/shard_map/ppermute | solution.py:338
  28.8 0.6 %subtract_bitcast_fusion = f32[1,8,512]{2,1,0:T(8,128)} fusion(f32[8,512]{1,0:T(8,128)S(1)} %get-tuple-element.51, f32[8,512]{1,0:T(8,128)S(1)} %collective-permute-done.5, f32[1,8,512]{2,1,0:T(8,128)S(1)} %copy-done), kind=kLoop, calls=%fused_computation.1 | loop fusion | flops 12288 | bytes 65536 | tf_op jit(solution)/shard_map/broadcast_in_dim | solution.py:416
  (1 shorter events, 0.0 us)
Async XLA Ops:
  0.6 9.8 %collective-permute-start = (f32[8,512]{1,0:T(8,128)}, f32[8,512]{1,0:T(8,128)S(1)}, u32[]{:S(2)}, u32[]{:S(2)}) collective-permute-start(f32[8,512]{1,0:T(8,128)} %bitcast.7), channel_id=1, source_target_pairs={{1,0},{0,1},{3,2},{2,3},{5,4},{4,5},{7,6},{6,7},{9,8},{8,9},{11,10... | collective-permute-start | bytes 49160 | tf_op jit(solution)/shard_map/ppermute | solution.py:338
  0.7 9.7 %collective-permute-start.1 = (f32[8,512]{1,0:T(8,128)}, f32[8,512]{1,0:T(8,128)S(1)}, u32[]{:S(2)}, u32[]{:S(2)}) collective-permute-start(f32[8,512]{1,0:T(8,128)} %bitcast.8), channel_id=1, source_target_pairs={{30,0},{31,1},{0,2},{1,3},{2,4},{3,5},{4,6},{5,7},{6,8},{7,9},{8,1... | collective-permute-start | bytes 49160 | tf_op jit(solution)/shard_map/ppermute | solution.py:338
  0.8 9.6 %collective-permute-start.2 = (f32[8,512]{1,0:T(8,128)}, f32[8,512]{1,0:T(8,128)S(1)}, u32[]{:S(2)}, u32[]{:S(2)}) collective-permute-start(f32[8,512]{1,0:T(8,128)} %bitcast.9), channel_id=1, source_target_pairs={{31,0},{2,1},{1,2},{4,3},{3,4},{6,5},{5,6},{8,7},{7,8},{10,9},{9,1... | collective-permute-start | bytes 49160 | tf_op jit(solution)/shard_map/ppermute | solution.py:338
  6.0 4.5 %collective-permute-start.3 = (f32[8,512]{1,0:T(8,128)}, f32[8,512]{1,0:T(8,128)S(1)}, u32[]{:S(2)}, u32[]{:S(2)}) collective-permute-start(f32[8,512]{1,0:T(8,128)} %bitcast.10), channel_id=1, source_target_pairs={{2,0},{3,1},{4,2},{5,3},{6,4},{7,5},{8,6},{9,7},{10,8},{11,9},{12,... | collective-permute-start | bytes 49160 | tf_op jit(solution)/shard_map/ppermute | solution.py:338
  8.4 2.1 %copy-start = (f32[1,8,512]{2,1,0:T(8,128)S(1)}, f32[1,8,512]{2,1,0:T(8,128)}, u32[]{:S(2)}) copy-start(f32[1,8,512]{2,1,0:T(8,128)} %param.7) | copy-start | bytes 49156
  10.5 10.4 %collective-permute-start.4 = (f32[24,512]{1,0:T(8,128)S(1)}, f32[24,512]{1,0:T(8,128)S(1)}, u32[]{:S(2)}, u32[]{:S(2)}) collective-permute-start(f32[24,512]{1,0:T(8,128)S(1)} %pad_maximum_fusion), channel_id=1, source_target_pairs={{32,0},{33,1},{34,2},{35,3},{36,4},{37,5},{38,6},{39,7},{40,8},{41... | collective-permute-start | bytes 147464 | tf_op jit(solution)/shard_map/ppermute | solution.py:338
  21.2 7.6 %collective-permute-start.5 = (f32[8,512]{1,0:T(8,128)S(1)}, f32[8,512]{1,0:T(8,128)S(1)}, u32[]{:S(2)}, u32[]{:S(2)}) collective-permute-start(f32[8,512]{1,0:T(8,128)S(1)} %get-tuple-element.52), channel_id=1, source_target_pairs={{224,0},{225,1},{226,2},{227,3},{228,4},{229,5},{230,6},{231,7},{2... | collective-permute-start | bytes 49160 | tf_op jit(solution)/shard_map/ppermute | solution.py:338
